TPU v7x, 128 devices: a whole 4x4x4 slice. The times are simulated.
128 devices in a mesh: clip: 4 (over y), space: 32 (over x, z, core).
Axes of the slice: x: 4, y: 4, z: 4, core: 2. Of those that a mesh axis runs over, the one named last changes fastest.
Arguments:
- frames: bfloat16 [4, 1024, 256, 256], P('clip', 'space'), may hold values from -6 to 6
- tail_frame: bfloat16 [1024, 256, 256], P('space'), may hold values from -6 to 6
- cotangent: bfloat16 [4, 1024, 2, 81, 256], P('clip', 'space'), may hold values from -6 to 6
- window_base: int32 [4, 1024, 2, 2, 256], P('clip', 'space'), may hold values from 4 to 10
- window_frac: bfloat16 [4, 1024, 2, 2, 256], P('clip', 'space'), may hold values from 0 to 1
- fine_owner: int32 [4, 1024, 1], P('clip'), may hold values from 0 to 31; in each aligned block of 32 rows (0 to 31, 32 to 63, ..., all dimensions but the last counted through in order) at most 2 rows name the same one
- fine_local: int32 [4, 1024], P('clip'), may hold values from 0 to 31
- coarse_owner: int32 [4, 1024, 1], P('clip'), may hold values from 0 to 31; in each aligned block of 32 rows (0 to 31, 32 to 63, ..., all dimensions but the last counted through in order) at most 2 rows name the same one
- coarse_block: int32 [4, 1024], P('clip'), may hold values from 0 to 1
Outputs:
- grad_first: bfloat16 [4, 1024, 256, 256], P('clip', 'space')
- grad_second: bfloat16 [4, 1024, 256, 256], P('clip', 'space')
Inputs may be any that keep to these rules, and one draw needn't show every extreme that they name: `fine_owner`: among the 32 query tiles of one device no device index is named more than 2 times, a bound that some block reaches. `coarse_owner`: among the 32 query tiles of one device no device index is named more than 2 times, a bound that some block reaches. `window_base`: every window lies inside its target tile.
All inputs are finite; a program needn't handle non-finite values.
Results may differ from a plain program's by a relative error of at most 0.0085.
Values may be sent and summed in bfloat16 or wider, within the bound.
A program may use at most 256 MiB of HBM per device.

v0:
```python
import math

import jax
import jax.numpy as jnp
from jax import lax
from jax.sharding import PartitionSpec as P

POOL = 4


def shifted_2(value, axis, steps):
    count = lax.axis_size(axis)
    first, last = (max(0, -steps), min(count, count - steps))
    return lax.ppermute(value, axis, [(source, source + steps) for source in range(first, last)])


def window_weights(base, fraction, tile_side, window_side):
    radius = window_side // 2
    offsets = jnp.arange(window_side, dtype=jnp.int32) - radius
    window_start = base[:, None, None, :] + offsets[None, :, None, None]
    column = jnp.arange(tile_side, dtype=jnp.int32)[None, None, :, None]
    at_lower = (column == window_start).astype(jnp.float32)
    at_upper = (column == window_start + 1).astype(jnp.float32)
    share = fraction[:, None, None, :]
    return (1.0 - share) * at_lower + share * at_upper


def window_grad(cotan, base, fraction):
    query_count = cotan.shape[0]
    pixels = cotan.shape[-1]
    tile_side = math.isqrt(pixels)
    window_side = math.isqrt(cotan.shape[1])
    values = cotan.astype(jnp.float32).reshape(query_count, window_side, window_side, pixels)
    cols_weight = window_weights(
        base[:, 0], fraction[:, 0].astype(jnp.float32), tile_side, window_side
    )
    rows_weight = window_weights(
        base[:, 1], fraction[:, 1].astype(jnp.float32), tile_side, window_side
    )
    partial_value = jnp.zeros((query_count, window_side, tile_side, pixels), jnp.float32)
    for shift_index in range(window_side):
        partial_value = (
            partial_value
            + values[:, :, shift_index, None, :] * cols_weight[:, shift_index, None, :, :]
        )
    window_map = jnp.zeros((query_count, tile_side, tile_side, pixels), jnp.float32)
    for shift_index in range(window_side):
        window_map = (
            window_map
            + rows_weight[:, shift_index, :, None, :] * partial_value[:, shift_index, None, :, :]
        )
    return window_map.reshape(query_count, pixels, pixels).astype(jnp.bfloat16)


def select_exact(form, selector, terms):
    upper = terms.astype(jnp.bfloat16)
    lower = (terms - upper.astype(jnp.float32)).astype(jnp.bfloat16)
    chooser = selector.astype(jnp.bfloat16)
    return jnp.einsum(form, chooser, upper, preferred_element_type=jnp.float32) + jnp.einsum(
        form, chooser, lower, preferred_element_type=jnp.float32
    )


def first_rows(target):
    matches = target[:, None] == target[None, :]
    ordinal = jnp.arange(target.shape[0])
    earlier = matches & (ordinal[None, :] < ordinal[:, None])
    leading = jnp.logical_not(jnp.any(earlier, axis=1))
    return (matches & leading[:, None]).astype(jnp.float32)


def combine(target, terms):
    return select_exact("ab,bjc->ajc", first_rows(target), terms)


def correlate(window_map, tiles, queries, norm_scale):
    query_grad = (
        jnp.einsum("qji,qjc->qic", window_map, tiles, preferred_element_type=jnp.float32)
        * norm_scale
    )
    toward = (
        jnp.einsum("qji,qic->qjc", window_map, queries, preferred_element_type=jnp.float32)
        * norm_scale
    )
    return (query_grad, toward)


def pooled_map(frame):
    tile_count, pixels, channels = frame.shape
    tile_side = math.isqrt(pixels)
    coarse_side = tile_side // POOL
    blocks = tile_count // (POOL * POOL)
    pieces = frame.reshape(blocks, POOL, POOL, coarse_side, POOL, coarse_side, POOL, channels)
    averages = jnp.sum(pieces, axis=(4, 6), dtype=jnp.float32) / (POOL * POOL)
    return (
        averages.transpose(0, 1, 3, 2, 4, 5).reshape(blocks, pixels, channels).astype(jnp.bfloat16)
    )


def spread_back(grads):
    blocks, pixels, channels = grads.shape
    tile_side = math.isqrt(pixels)
    coarse_side = tile_side // POOL
    pieces = grads.reshape(blocks, POOL, coarse_side, POOL, coarse_side, channels).transpose(
        0, 1, 3, 2, 4, 5
    )
    expanded = jnp.broadcast_to(
        pieces[:, :, :, :, None, :, None, :],
        (blocks, POOL, POOL, coarse_side, POOL, coarse_side, POOL, channels),
    ) / (POOL * POOL)
    return expanded.reshape(blocks * POOL * POOL, pixels, channels)


def slot_plan(owner_rows, local_rows, spaces, position, capacity):
    owners = owner_rows.reshape(spaces, -1)
    local_ids = local_rows.reshape(spaces, -1)
    per_device = owners.shape[1]
    matches = owners[:, :, None] == owners[:, None, :]
    ordinal = jnp.arange(per_device)
    ranking = jnp.sum(matches & (ordinal[None, None, :] < ordinal[None, :, None]), axis=2)
    flat_slot = jnp.arange(spaces, dtype=jnp.int32)[:, None] * capacity + ranking
    flat_slot = jnp.where(owners == position, flat_slot, spaces * capacity)
    served = (
        jnp.zeros((spaces * capacity,), jnp.int32)
        .at[flat_slot.reshape(-1)]
        .set(local_ids.reshape(-1), mode="drop")
    )
    my_owner = lax.dynamic_index_in_dim(owners, position, 0, keepdims=False)
    my_ranking = lax.dynamic_index_in_dim(ranking, position, 0, keepdims=False)
    my_local = lax.dynamic_index_in_dim(local_ids, position, 0, keepdims=False)
    return (served, my_owner * capacity + my_ranking, my_owner, my_local)


def body(
    frames,
    tail_frame,
    cotangent,
    window_base,
    window_frac,
    fine_owner,
    fine_local,
    coarse_owner,
    coarse_block,
):
    first_tiles = frames[0]
    tile_count, pixels, channels = first_tiles.shape
    shifted = shifted_2(frames, "clip", -1)
    at_end = lax.axis_index("clip") == lax.axis_size("clip") - 1
    second_tiles = jnp.where(at_end, tail_frame, shifted[0])
    spaces = lax.axis_size("space")
    position = lax.axis_index("space")
    capacity = max(2, 2 * tile_count // spaces)
    blocks = tile_count // (POOL * POOL)
    norm_scale = 1.0 / math.sqrt(channels)
    cot_fine = cotangent[0, :, 0]
    base_fine = window_base[0, :, 0]
    frac_fine = window_frac[0, :, 0]
    served, my_slots, my_owner, my_local = slot_plan(
        fine_owner[0, :, 0], fine_local[0], spaces, position, capacity
    )
    fine_target = my_owner * tile_count + my_local
    selector = (jnp.arange(tile_count, dtype=jnp.int32)[:, None] == served[None, :]).astype(
        jnp.bfloat16
    )
    outgoing = jnp.take(second_tiles, served, axis=0).reshape(spaces, capacity, pixels, channels)
    received = lax.all_to_all(outgoing, "space", split_axis=0, concat_axis=0, tiled=True)
    fine_tiles = jnp.take(received.reshape(spaces * capacity, pixels, channels), my_slots, axis=0)
    fine_map = window_grad(cot_fine, base_fine, frac_fine)
    fine_back, fine_toward = correlate(fine_map, fine_tiles, first_tiles, norm_scale)
    fine_back = lax.optimization_barrier(fine_back.astype(jnp.bfloat16)).astype(jnp.float32)
    fine_part = combine(fine_target, fine_toward).astype(jnp.bfloat16)
    returning = (
        jnp.zeros((spaces * capacity, pixels, channels), jnp.bfloat16).at[my_slots].set(fine_part)
    )
    returned = lax.all_to_all(
        returning.reshape(spaces, capacity, pixels, channels),
        "space",
        split_axis=0,
        concat_axis=0,
        tiled=True,
    )
    fine_grad = jnp.einsum(
        "ts,sjc->tjc",
        selector,
        returned.reshape(spaces * capacity, pixels, channels),
        preferred_element_type=jnp.float32,
    )
    pooled = pooled_map(second_tiles)
    coarse_owners = coarse_owner[0, :, 0]
    coarse_blocks = coarse_block[0]
    my_coarse_owner = lax.dynamic_slice_in_dim(coarse_owners, position * tile_count, tile_count)
    my_coarse_block = lax.dynamic_slice_in_dim(coarse_blocks, position * tile_count, tile_count)
    coarse_target = my_coarse_owner * blocks + my_coarse_block
    coarse_map = window_grad(cotangent[0, :, 1], window_base[0, :, 1], window_frac[0, :, 1])
    coarse_all = lax.all_gather(pooled, "space", axis=0, tiled=True)
    coarse_tiles = jnp.take(coarse_all, coarse_target, axis=0)
    coarse_back, coarse_toward = correlate(coarse_map, coarse_tiles, first_tiles, norm_scale)
    matches = (
        jnp.arange(lax.axis_size("space") * blocks, dtype=jnp.int32)[:, None]
        == coarse_target[None, :]
    ).astype(jnp.float32)
    coarse_grad = lax.psum_scatter(
        select_exact("ab,bjc->ajc", matches, coarse_toward).astype(jnp.bfloat16),
        "space",
        scatter_dimension=0,
        tiled=True,
    ).astype(jnp.float32)
    grad_first = (fine_back + coarse_back).astype(jnp.bfloat16)
    grad_second = (fine_grad + spread_back(coarse_grad)).astype(jnp.bfloat16)
    return (grad_first[None], grad_second[None])


def solution(mesh):
    in_specs = (
        P("clip", "space", None, None),
        P("space", None, None),
        P("clip", "space", None, None, None),
        P("clip", "space", None, None, None),
        P("clip", "space", None, None, None),
        P("clip", None, None),
        P("clip", None),
        P("clip", None, None),
        P("clip", None),
    )
    out_specs = (P("clip", "space", None, None), P("clip", "space", None, None))
    return jax.shard_map(body, mesh=mesh, in_specs=in_specs, out_specs=out_specs, check_vma=False)
```

profile of v0, /device:TPU:56, one launch (start us, length us, event | category | flops | bytes accessed | tf_op | source)
XLA Modules:
  0.0 504.0 jit_solution(4878455551409297208)
XLA Ops:
  29.1 12.3 %add_convert_fusion.1 = bf16[32,16,16,256]{3,2,1,0:T(8,128)(2,1)S(1)} fusion(f32[32,16,256]{2,1,0:T(8,128)S(1)} %get-tuple-element.31, f32[32,16,256]{2,1,0:T(8,128)} %get-tuple-element.22, f32[32,16,256]{2,1,0:T(8,128)S(1)} %get-tuple-element.32, f32[32,16,256]{2,1,0:T(8,128)} %get-tuple-element.23, f32[32,16,256]{2,1,0:T(8,128)S(1)} %get-tuple-element.33, ...), kind=kLoop, calls=%fused_computation.6 | loop fusion | flops 37748736 | bytes 13631488 | tf_op jit(solution)/shard_map/convert_element_type | solution.py:52
  48.9 11.0 %fusion.7 = f32[64,256,256]{2,0,1:T(8,128)} fusion(bf16[32,256,256]{2,1,0:T(8,128)(2,1)} %get-tuple-element.20, s32[32]{0:T(128)S(1)} %fusion.54), kind=kOutput, calls=%fused_computation.39 | convolution fusion | flops 268441600 | bytes 20971648 | tf_op jit(solution)/shard_map/ab,bjc->ajc/dot_general | solution.py:59
  59.9 15.0 %add_convert_fusion = bf16[64,256,256]{2,0,1:T(8,128)(2,1)} fusion(f32[64,256,256]{2,0,1:T(8,128)} %fusion.7, bf16[32,256,256]{2,1,0:T(8,128)(2,1)S(1)} %copy-done.4, s32[32]{0:T(128)S(1)} %fusion.54), kind=kOutput, calls=%fused_computation.5 | convolution fusion | flops 276830208 | bytes 29360256 | tf_op jit(solution)/shard_map/ab,bjc->ajc/dot_general | solution.py:59
  74.9 11.4 %copy.102 = bf16[64,256,256]{2,1,0:T(8,128)(2,1)} copy(bf16[64,256,256]{2,0,1:T(8,128)(2,1)} %add_convert_fusion) | data formatting | bytes 16777216 | tf_op jit(solution)/shard_map/convert_element_type | solution.py:203
  103.5 10.4 %add_convert_fusion.2 = bf16[32,16,16,256]{3,2,1,0:T(8,128)(2,1)S(1)} fusion(f32[32,16,256]{2,1,0:T(8,128)S(1)} %get-tuple-element.58, f32[32,16,256]{2,1,0:T(8,128)S(1)} %get-tuple-element.49, f32[32,16,256]{2,1,0:T(8,128)S(1)} %get-tuple-element.59, f32[32,16,256]{2,1,0:T(8,128)S(1)} %get-tuple-element.50, f32[32,16,256]{2,1,0:T(8,128)S(1)} %get-tuple-element.60, ...), kind=kLoop, calls=%fused_computation.7 | loop fusion | flops 37748736 | bytes 13631488 | tf_op jit(solution)/shard_map/convert_element_type | solution.py:52
  130.8 11.5 %scatter_fusion = bf16[64,256,256]{2,1,0:T(8,128)(2,1)} fusion(bf16[64,256,256]{2,1,0:T(8,128)(2,1)} %broadcast_in_dim.44, s32[32]{0:T(128)S(1)} %get-tuple-element.13, bf16[32,256,256]{2,1,0:T(8,128)(2,1)} %copy.97), kind=kCustom, calls=%fused_computation.4 | custom fusion | bytes 12583040 | tf_op jit(solution)/shard_map/scatter | solution.py:173
  142.3 16.3 %copy.98 = bf16[32,2,256,256]{3,1,2,0:T(2,128)(2,1)} copy(bf16[32,2,256,256]{3,2,1,0:T(8,128)(2,1)} %bitcast.270) | data formatting | bytes 16777216 | tf_op jit(solution)/shard_map/reshape | solution.py:176
  158.6 8.7 %all-to-all-start.1 = ((bf16[32,2,256,256]{3,1,2,0:T(2,128)(2,1)}), bf16[32,2,256,256]{3,1,2,0:T(2,128)(2,1)}, u32[]{:S(2)}, u32[]{:S(2)}) async-start(bf16[32,2,256,256]{3,1,2,0:T(2,128)(2,1)} %copy.98), calls=%async_computation.1 | async-start | bytes 16777216 | tf_op jit(solution)/shard_map/all_to_all | solution.py:175
  167.4 12.0 %collective-permute-done = bf16[1,32,256,256]{3,2,1,0:T(8,128)(2,1)} collective-permute-done((bf16[1,32,256,256]{3,2,1,0:T(8,128)(2,1)}, bf16[1,32,256,256]{3,2,1,0:T(8,128)(2,1)}, u32[]{:S(2)}, u32[]{:S(2)}) %collective-permute-start) | collective-permute-done | bytes 4194336 | tf_op jit(solution)/shard_map/ppermute | solution.py:14
  185.3 8.1 %reshape.357 = f32[2,4,4,4,4,4,4,256]{7,6,5,4,3,2,1,0:T(4,128)} reshape(bf16[32,256,256]{2,1,0:T(8,128)(2,1)} %bitcast_select_fusion) | data formatting | bytes 12582912 | tf_op jit(solution)/shard_map/convert_element_type | solution.py:94
  193.4 6.7 %reduce_sum.19 = f32[2,4,4,4,4,256]{5,4,3,2,1,0:T(4,128)S(1)} reduce(f32[2,4,4,4,4,4,4,256]{7,6,5,4,3,2,1,0:T(4,128)} %reshape.357, f32[]{:T(128)} %constant.43.clone.1), dimensions={4,6}, to_apply=%region_2.4 | reduce | flops 1966080 | bytes 8912900 | tf_op jit(solution)/shard_map/reduce_sum | solution.py:94
  205.9 7.6 %gather_fusion = bf16[64,256,256]{2,1,0:T(8,128)(2,1)} fusion(bf16[32,256,256]{2,1,0:T(8,128)(2,1)} %bitcast_select_fusion, s32[1024]{0:T(1024)S(1)} %pad_clamp_fusion.2), kind=kCustom, calls=%fused_computation.2 | custom fusion | bytes 16777472 | tf_op jit(solution)/shard_map/jit(_take)/gather | solution.py:165
  213.4 7.5 %broadcast_select_fusion = bf16[32,2,256,256]{3,2,1,0:T(8,128)(2,1)} fusion(bf16[32,2,256,256]{3,2,1,0:T(8,128)(2,1)} %bitcast.271, pred[32,2]{1,0:T(8,128)(4,1)S(1)} %broadcast_in_dim.39), kind=kLoop, calls=%fused_computation.14 | loop fusion | flops 4194304 | bytes 16777280 | tf_op jit(solution)/shard_map/jit(_take)/select_n | solution.py:165
  220.9 87.8 %all-to-all-done.1 = bf16[32,2,256,256]{3,1,2,0:T(2,128)(2,1)} async-done(((bf16[32,2,256,256]{3,1,2,0:T(2,128)(2,1)}), bf16[32,2,256,256]{3,1,2,0:T(2,128)(2,1)}, u32[]{:S(2)}, u32[]{:S(2)}) %all-to-all-start.1) | async-done | bytes 8388640 | tf_op jit(solution)/shard_map/all_to_all | solution.py:175
  308.8 7.4 %all-to-all-start = ((bf16[32,2,256,256]{3,2,1,0:T(8,128)(2,1)}), bf16[32,2,256,256]{3,2,1,0:T(8,128)(2,1)}, u32[]{:S(2)}, u32[]{:S(2)}) async-start(bf16[32,2,256,256]{3,2,1,0:T(8,128)(2,1)} %broadcast_select_fusion), calls=%async_computation | async-start | bytes 16777216 | tf_op jit(solution)/shard_map/all_to_all | solution.py:166
  317.0 10.0 %copy.99 = bf16[32,2,256,256]{3,1,0,2:T(2,128)(2,1)} copy(bf16[32,2,256,256]{3,1,2,0:T(2,128)(2,1)} %all-to-all-done.1) | data formatting | bytes 16777216 | tf_op jit(solution)/shard_map/all_to_all | solution.py:175
  326.9 13.1 %reshape.347 = bf16[64,256,256]{2,0,1:T(8,128)(2,1)} reshape(bf16[32,2,256,256]{3,1,0,2:T(2,128)(2,1)} %copy.99) | data formatting | bytes 16777216 | tf_op jit(solution)/shard_map/reshape | solution.py:185
  340.0 100.0 %all-to-all-done = bf16[32,2,256,256]{3,2,1,0:T(8,128)(2,1)} async-done(((bf16[32,2,256,256]{3,2,1,0:T(8,128)(2,1)}), bf16[32,2,256,256]{3,2,1,0:T(8,128)(2,1)}, u32[]{:S(2)}, u32[]{:S(2)}) %all-to-all-start) | async-done | bytes 8388640 | tf_op jit(solution)/shard_map/all_to_all | solution.py:166
  440.1 6.2 %gather_fusion.1 = bf16[32,256,256]{2,1,0:T(8,128)(2,1)} fusion(bf16[64,256,256]{2,1,0:T(8,128)(2,1)} %bitcast.51, s32[1024]{0:T(1024)S(1)} %pad_clamp_fusion.1), kind=kCustom, calls=%fused_computation.clone | custom fusion | bytes 8388736 | tf_op jit(solution)/shard_map/jit(_take)/gather | solution.py:167
  446.3 7.3 %multiply_convert_fusion = bf16[32,256,256]{2,1,0:T(8,128)(2,1)} fusion(bf16[32,256,256]{2,1,0:T(8,128)(2,1)} %bitcast.275, bf16[32,256,256]{2,1,0:T(8,128)(2,1)} %gather_fusion.1, pred[32]{0:T(512)(128)(4,1)S(1)} %compare_and_fusion.3), kind=kOutput, calls=%fused_computation.13 | convolution fusion | flops 1080033280 | bytes 12582944 | tf_op jit(solution)/shard_map/qji,qjc->qic/dot_general | solution.py:78
  460.3 10.1 %reshape.348 = f32[32,256,256]{2,0,1:T(8,128)} reshape(f32[2,4,4,4,4,4,4,256]{7,2,1,0,6,5,4,3:T(4,128)} %broadcast_in_dim.45) | data formatting | bytes 16777216 | tf_op jit(solution)/shard_map/reshape | solution.py:111
  470.4 7.1 %fusion.1 = bf16[1,32,256,256]{3,1,2,0:T(8,128)(2,1)S(1)} fusion(f32[32,256,256]{2,0,1:T(8,128)} %reshape.348, bf16[64,256,256]{2,0,1:T(8,128)(2,1)} %reshape.347, s32[64]{0:T(128)S(1)} %scatter_custom_fusion), kind=kOutput, calls=%fused_computation.32 | convolution fusion | flops 272631808 | bytes 20971776 | tf_op jit(solution)/shard_map/ts,sjc->tjc/dot_general | solution.py:182
  481.8 6.1 %gather_fusion.2 = bf16[32,256,256]{2,1,0:T(8,128)(2,1)} fusion(bf16[64,256,256]{2,1,0:T(8,128)(2,1)} %all-gather.2.cloned.1.call-done, s32[1024]{0:T(1024)S(1)} %pad_clamp_fusion), kind=kCustom, calls=%fused_computation.1.clone | custom fusion | bytes 8388736 | tf_op jit(solution)/shard_map/jit(_take)/gather | solution.py:196
  488.0 8.8 %fusion = bf16[1,32,256,256]{3,2,1,0:T(8,128)(2,1)} fusion(bf16[32,256,256]{2,1,0:T(8,128)(2,1)} %multiply_convert_fusion, bf16[32,256,256]{2,1,0:T(8,128)(2,1)} %bitcast.273, bf16[32,256,256]{2,1,0:T(8,128)(2,1)} %gather_fusion.2, pred[32]{0:T(512)(128)(4,1)S(1)} %get-tuple-element.15), kind=kOutput, calls=%fused_computation.31 | convolution fusion | flops 1084227584 | bytes 16777248 | tf_op jit(solution)/shard_map/qji,qjc->qic/dot_general | solution.py:78
  (105 shorter events, 86.7 us)
Async XLA Ops:
  7.2 446.4 %reduce-scatter.2.cloned.1.call-start = ((), (), s32[]{:S(2)}) async-start(), calls=%async_computation.4 | async-start | bytes 8650752 | tf_op jit(solution)/shard_map/reduce_scatter | solution.py:202
  12.3 1.8 copy-start.5
  19.6 1.0 copy-start.7
  29.1 14.4 %copy-start.2 = (bf16[1,32,256,256]{3,2,1,0:T(8,128)(2,1)S(1)}, bf16[1,32,256,256]{3,2,1,0:T(8,128)(2,1)}, u32[]{:S(2)}) copy-start(bf16[1,32,256,256]{3,2,1,0:T(8,128)(2,1)} %param.11) | copy-start | bytes 12582916
  41.4 2.1 copy-start
  48.9 11.0 %copy-start.4 = (bf16[32,256,256]{2,1,0:T(8,128)(2,1)S(1)}, bf16[32,256,256]{2,1,0:T(8,128)(2,1)}, u32[]{:S(2)}) copy-start(bf16[32,256,256]{2,1,0:T(8,128)(2,1)} %get-tuple-element.19) | copy-start | bytes 12582916
  86.3 5.1 %copy-start.6 = (bf16[1,32,1,81,256]{4,2,3,1,0:T(2,128)(2,1)S(1)}, bf16[1,32,1,81,256]{4,2,3,1,0:T(2,128)(2,1)}, u32[]{:S(2)}) copy-start(bf16[1,32,1,81,256]{4,2,3,1,0:T(2,128)(2,1)} %get-tuple-element.85) | copy-start | bytes 3981316
  86.3 6.2 %copy-start.9 = (s32[1,1024,1]{1,2,0:T(1,128)S(1)}, s32[1,1024,1]{1,2,0:T(1,128)}, u32[]{:S(2)}) copy-start(s32[1,1024,1]{1,2,0:T(1,128)} %param.16) | copy-start | bytes 12292
  86.3 6.9 %copy-start.10 = (s32[1,1024]{1,0:T(1,128)S(1)}, s32[1,1024]{1,0:T(1,128)}, u32[]{:S(2)}) copy-start(s32[1,1024]{1,0:T(1,128)} %param.17) | copy-start | bytes 12292
  86.3 93.1 %collective-permute-start = (bf16[1,32,256,256]{3,2,1,0:T(8,128)(2,1)}, bf16[1,32,256,256]{3,2,1,0:T(8,128)(2,1)}, u32[]{:S(2)}, u32[]{:S(2)}) collective-permute-start(bf16[1,32,256,256]{3,2,1,0:T(8,128)(2,1)} %param.11), channel_id=1, source_target_pairs={{32,0},{64,32},{96,64},{33,1},{65,33},{97,65},{34,2},{66,34},{98,6... | collective-permute-start | bytes 12582920 | tf_op jit(solution)/shard_map/ppermute | solution.py:14
  91.6 2.8 copy-start.8
  103.4 10.5 %copy-start.3 = (bf16[1,32,256,256]{3,2,1,0:T(8,128)(2,1)S(1)}, bf16[1,32,256,256]{3,2,1,0:T(8,128)(2,1)}, u32[]{:S(2)}) copy-start(bf16[1,32,256,256]{3,2,1,0:T(8,128)(2,1)} %param.11) | copy-start | bytes 12582916
  113.9 2.0 copy-start.1
  158.6 150.2 %all-to-all-start.1 = ((bf16[32,2,256,256]{3,1,2,0:T(2,128)(2,1)}), bf16[32,2,256,256]{3,1,2,0:T(2,128)(2,1)}, u32[]{:S(2)}, u32[]{:S(2)}) async-start(bf16[32,2,256,256]{3,1,2,0:T(2,128)(2,1)} %copy.98), calls=%async_computation.1 | async-start | bytes 16777216 | tf_op jit(solution)/shard_map/all_to_all | solution.py:175
  167.3 314.5 %all-gather.2.cloned.1.call-start = ((), (), s32[]{:S(2)}) async-start(), calls=%async_computation.3 | async-start | bytes 8650752 | tf_op jit(solution)/shard_map/all_gather | solution.py:195
  308.8 131.3 %all-to-all-start = ((bf16[32,2,256,256]{3,2,1,0:T(8,128)(2,1)}), bf16[32,2,256,256]{3,2,1,0:T(8,128)(2,1)}, u32[]{:S(2)}, u32[]{:S(2)}) async-start(bf16[32,2,256,256]{3,2,1,0:T(8,128)(2,1)} %broadcast_select_fusion), calls=%async_computation | async-start | bytes 16777216 | tf_op jit(solution)/shard_map/all_to_all | solution.py:166
Sparse Core Ops, SparseCore 0:
  86.4 131.7 reduce-scatter.1
  220.7 95.6 all-gather.1
where the time goes:
time: 514 us; the launch traced here: 504 us
  waiting for transfers between devices  200 us (39%)
  local copies, waits for them, and re-layouts  144 us (28%)
  other arithmetic  63.7 us (12%)
  matrix products  60.5 us (12%)
  starting transfers between devices  21.2 us (4%)
  between operations  15 us (3%)
    all_to_all x1, waiting for transfers between devices, body(): lax.all_to_all(outgoing, 'space', split_axis=0, concat_axis=0, tiled=True)  100 us
    all_to_all x1, waiting for transfers between devices, body(): lax.all_to_all(returning.reshape(spaces, capacity, pixels, channels), 'sp...  87.8 us
    convert_element_type x2, other arithmetic, window_grad(): return window_map.reshape(query_count, pixels, pixels).astype(jnp.bfloat16)  22.8 us
    dot_general x2, matrix products, select_exact(): jnp.einsum(form, chooser, lower, preferred_element_type=jnp.float32)  17.6 us
    reshape x1, local copies, waits for them, and re-layouts, body(): returning.reshape(spaces, capacity, pixels, channels)  16.3 us
    dot_general x2, matrix products, correlate(): jnp.einsum('qji,qjc->qic', window_map, tiles, preferred_element_type=jnp....  16.1 us
    dot_general x2, matrix products, select_exact(): jnp.einsum(form, chooser, upper, preferred_element_type=jnp.float32)  13.8 us
    reshape x1, local copies, waits for them, and re-layouts, body(): returned.reshape(spaces * capacity, pixels, channels)  13.1 us
  transfers between devices with their start and end apart: 5, of which 3 were waited for; matrix products, arithmetic and copies ran while one was open for 34% of the time, Pallas kernels for 0%

commit v1 on v0

v1 whole, which is shorter than its diff:
```python
import functools
import math

import jax
import jax.numpy as jnp
import numpy as np
from jax import lax
from jax.experimental import pallas as pl
from jax.experimental.pallas import tpu as pltpu
from jax.sharding import PartitionSpec as P

MESH = pl.DeviceIdType.MESH
POOL = 4
SIDE = 16
WIN = 9
PIX = 256
HALF = PIX // 2
NX, NZ, NC = 4, 4, 2
BLK = 2
TILES = 32
SLOTS = 2 * TILES
F32 = jnp.float32
BF16 = jnp.bfloat16


def placement():
    spread = np.zeros((2 * WIN * SIDE, WIN * WIN), np.float32)
    for a in range(WIN):
        for k in range(WIN):
            spread[a * SIDE + k, a * WIN + k] = 1
            spread[WIN * SIDE + a * SIDE + k + 1, a * WIN + k] = 1
    return spread


def pool_rows():
    rows = np.zeros((SIDE, PIX), np.float32)
    for y in range(SIDE):
        for x in range(SIDE):
            rows[(y // POOL) * POOL + x // POOL, y * SIDE + x] = 1
    return rows


def block_rows():
    rows = np.zeros((PIX, PIX), np.float32)
    for ty in range(4):
        for tx in range(4):
            for a in range(4):
                for b in range(4):
                    rows[(ty * 4 + a) * 16 + tx * 4 + b, (ty * 4 + tx) * 16 + a * 4 + b] = 1
    return rows


def dot(a, b):
    return jnp.dot(a, b, preferred_element_type=F32)


def window_map(spread, cot, base, frac):
    placed = dot(spread, cot)
    rows = WIN * SIDE
    fx = frac[0:1].astype(F32)
    fy = frac[1:2].astype(F32)
    shape = (SIDE, PIX)
    ox = jnp.broadcast_to(base[0:1] - WIN // 2, shape)
    oy = jnp.broadcast_to(base[1:2] - WIN // 2, shape)
    across = (1.0 - fx) * placed[:rows] + fx * placed[rows:]
    groups = []
    for y in range(WIN + 1):
        value = None
        if y < WIN:
            value = (1.0 - fy) * across[y * SIDE : (y + 1) * SIDE]
        if y > 0:
            below = fy * across[(y - 1) * SIDE : y * SIDE]
            value = below if value is None else value + below
        groups.append(value)
    for step in (1, 2, 4):
        chosen = (ox & step) != 0
        groups = [jnp.where(chosen, pltpu.roll(g, step, 0), g) for g in groups]
    zero = jnp.zeros(shape, F32)
    for step in (1, 2, 4):
        chosen = (oy & step) != 0
        count = min(SIDE, len(groups) + step)
        groups = [
            jnp.where(
                chosen,
                groups[y - step] if y >= step else zero,
                groups[y] if y < len(groups) else zero,
            )
            for y in range(count)
        ]
    return jnp.concatenate(groups, axis=0).astype(BF16)


def prep_kernel(
    slot_ref, spread_ref, pool_ref, perm_ref, cot_ref, base_ref, frac_ref, frame_ref, tail_ref,
    fine_ref, coarse_ref, ret_ref, terms_ref, pooled_ref, raw
):
    step = pl.program_id(0)
    scale = 1.0 / 16.0
    frame = frame_ref[0]
    fine = window_map(spread_ref[...], cot_ref[0, 0], base_ref[0, 0], frac_ref[0, 0])
    fine_ref[0] = fine
    ret_ref[0] = (dot(fine, frame) * scale).astype(BF16)
    coarse = window_map(spread_ref[...], cot_ref[0, 1], base_ref[0, 1], frac_ref[0, 1])
    coarse_ref[0] = coarse
    terms_ref[0] = (dot(coarse, frame) * scale).astype(BF16)
    rows = pl.ds(pl.multiple_of((step % 16) * SIDE, SIDE), SIDE)
    block = step // 16
    raw[0, block, rows, :] = (dot(pool_ref[...], frame) * scale).astype(BF16)
    raw[1, block, rows, :] = (dot(pool_ref[...], tail_ref[0]) * scale).astype(BF16)

    @pl.when(step == TILES - 1)
    def _():
        for which in range(2):
            for b in range(BLK):
                pooled_ref[which, b] = dot(perm_ref[...], raw[which, b]).astype(BF16)


def prep(slots, cot, base, frac, frames, tail):
    tile = lambda q, s: (q, 0, 0)
    whole = lambda q, s: (0, 0)
    four = lambda q, s: (q, 0, 0, 0)
    one = (1, PIX, PIX)
    out = jax.ShapeDtypeStruct((TILES, PIX, PIX), BF16)
    return pl.pallas_call(
        prep_kernel,
        grid_spec=pltpu.PrefetchScalarGridSpec(
            num_scalar_prefetch=1,
            grid=(TILES,),
            in_specs=[
                pl.BlockSpec((2 * WIN * SIDE, WIN * WIN), whole),
                pl.BlockSpec((SIDE, PIX), whole),
                pl.BlockSpec((PIX, PIX), whole),
                pl.BlockSpec((1, 2, WIN * WIN, PIX), four),
                pl.BlockSpec((1, 2, 2, PIX), four),
                pl.BlockSpec((1, 2, 2, PIX), four),
                pl.BlockSpec(one, tile),
                pl.BlockSpec(one, tile),
            ],
            out_specs=[
                pl.BlockSpec(one, tile),
                pl.BlockSpec(one, tile),
                pl.BlockSpec(one, lambda q, s: (s[q], 0, 0)),
                pl.BlockSpec(one, tile),
                pl.BlockSpec((2, BLK, PIX, PIX), lambda q, s: (0, 0, 0, 0)),
            ],
            scratch_shapes=[pltpu.VMEM((2, BLK, PIX, PIX), BF16)],
        ),
        out_shape=[out, out, jax.ShapeDtypeStruct((SLOTS, PIX, PIX), BF16), out,
                   jax.ShapeDtypeStruct((2, BLK, PIX, PIX), BF16)],
        compiler_params=pltpu.CompilerParams(vmem_limit_bytes=40 * 2**20),
        name="prep",
    )(slots, jnp.asarray(placement(), BF16), jnp.asarray(pool_rows(), BF16),
      jnp.asarray(block_rows(), BF16), cot, base, frac, frames, tail)


def exchange_kernel(
    served_ref, pick_a, pick_b, frames, tail, ret, terms, pooled,
    got, back, every, coarse_ref, ret_a, ret_b, get_a, get_b,
    tiles, fetch, own, partial, sibling, pbuf,
    red_a, red_b, mid_a, mid_b, last_a, last_b, coarse,
    send, recv, local
):
    clip = lax.axis_index("clip")
    space = lax.axis_index("space")
    x = space // (NZ * NC)
    z = (space // NC) % NZ
    c = space % NC
    counts = {"remote": 0, "local": 0}

    def along_x(d, core=0):
        return (clip, (((x + d) % NX) * NZ + z) * NC + (c + core) % NC)

    def along_z(d, core=0):
        return (clip, (x * NZ + (z + d) % NZ) * NC + (c + core) % NC)

    def remote(src, dst, device):
        n = counts["remote"]
        counts["remote"] += 1
        return pltpu.make_async_remote_copy(
            src_ref=src, dst_ref=dst, send_sem=send.at[n], recv_sem=recv.at[n],
            device_id=device, device_id_type=MESH)

    def here(src, dst):
        n = counts["local"]
        counts["local"] += 1
        return pltpu.make_async_copy(src, dst, local.at[n])

    def start(copies):
        for copy in copies:
            copy.start()
        return copies

    def arrive(copies):
        for copy in copies:
            copy.wait_recv()

    barrier = pltpu.get_barrier_semaphore()
    greeted = [along_x(d, k) for d in range(1, NX) for k in range(NC)]
    greeted += [along_z(d, k) for d in range(1, NZ) for k in range(NC)]
    greeted += [along_x(0, 1), ((clip + 1) % 4, space)]
    for device in greeted:
        pl.semaphore_signal(barrier, inc=1, device_id=device, device_id_type=MESH)
    pl.semaphore_wait(barrier, len(greeted))

    sent = []
    at_end = clip == 3
    below = ((clip + 3) % 4, space)
    move_pool = remote(pooled.at[0], pbuf, below)
    move_tiles = remote(frames, tiles, below)
    end_pool = here(pooled.at[1], pbuf)
    end_tiles = here(tail, tiles)

    @pl.when(clip > 0)
    def _():
        move_pool.start()
        move_tiles.start()

    @pl.when(at_end)
    def _():
        end_pool.start()
        end_tiles.start()

    load_terms = start([here(terms, own.at[pl.ds(0, TILES)])])

    keep_a = start([here(ret.at[0, x], ret_a.at[:, :, x])])
    keep_b = start([here(ret.at[1, z], ret_b.at[:, :, z])])
    ret_a1 = start([remote(ret.at[0, (x + d) % NX], ret_a.at[:, :, x], along_x(d)) for d in range(1, NX)])
    ret_b1 = start([remote(ret.at[1, (z + d) % NZ], ret_b.at[:, :, z], along_z(d)) for d in range(1, NZ)])
    sent += ret_a1 + ret_b1

    own[TILES] = jnp.zeros((PIX, PIX), BF16)
    for copy in load_terms:
        copy.wait()

    def picked(n):
        first = own[pick_a[n]].astype(F32)
        return (first + own[pick_b[n]].astype(F32)).astype(BF16)

    def fill(which, core):
        def one(n, carry):
            partial[which, n // (NZ * BLK), (n // BLK) % NZ, n % BLK] = picked(core * TILES + n)
            return carry
        lax.fori_loop(0, TILES, one, 0)

    fill(1, 1 - c)
    share = start([remote(partial.at[1], sibling, along_x(0, 1))])
    sent += share
    fill(0, c)

    @pl.when(at_end)
    def _():
        end_pool.wait()

    @pl.when(clip < 3)
    def _():
        move_pool.wait_recv()

    top, bottom = pl.ds(0, HALF), pl.ds(HALF, HALF)
    keep_pool = start([here(pbuf, every.at[c, x, z])])
    pool_a1 = start([remote(pbuf.at[:, top], every.at[c, x, z, :, top], along_x(d)) for d in range(1, NX)])
    pool_b1 = start([remote(pbuf.at[:, bottom], every.at[c, x, z, :, bottom], along_z(d)) for d in range(1, NZ)])
    sent += pool_a1 + pool_b1

    arrive(share)

    def join(n, carry):
        at = (n // (NZ * BLK), (n // BLK) % NZ, n % BLK)
        mine = partial[(0, *at)].astype(F32)
        partial[(0, *at)] = (mine + sibling[at].astype(F32)).astype(BF16)
        return carry

    lax.fori_loop(0, TILES, join, 0)
    mine = partial.at[0]
    red_a1 = start([remote(mine.at[:, (z + d) % NZ, :, top], red_a.at[z], along_z(d)) for d in range(1, NZ)])
    red_b1 = start([remote(mine.at[(x + d) % NX, :, :, bottom], red_b.at[x], along_x(d)) for d in range(1, NX)])
    sent += red_a1 + red_b1

    def store_own_a(n, carry):
        red_a[z, n // BLK, n % BLK] = partial[0, n // BLK, z, n % BLK, top]
        red_b[x, n // BLK, n % BLK] = partial[0, x, n // BLK, n % BLK, bottom]
        return carry

    lax.fori_loop(0, NX * BLK, store_own_a, 0)

    for copy in keep_pool:
        copy.wait()
    arrive(pool_a1)
    pool_a2 = start([remote(every.at[c, :, z, :, top], every.at[c, :, z, :, top], along_z(d)) for d in range(1, NZ)])
    arrive(pool_b1)
    pool_b2 = start([remote(every.at[c, x, :, :, bottom], every.at[c, x, :, :, bottom], along_x(d)) for d in range(1, NX)])
    sent += pool_a2 + pool_b2

    def total(buffer, at):
        value = buffer[(0, *at)].astype(F32)
        for n in range(1, 4):
            value = value + buffer[(n, *at)].astype(F32)
        return value

    arrive(red_a1)
    arrive(red_b1)

    def middle(n, carry):
        at = (n // BLK, n % BLK)
        mid_a[at] = total(red_a, at).astype(BF16)
        mid_b[at] = total(red_b, at).astype(BF16)
        return carry

    lax.fori_loop(0, NX * BLK, middle, 0)
    red_a2 = start([remote(mid_a.at[(x + d) % NX], last_a.at[x], along_x(d)) for d in range(1, NX)])
    red_b2 = start([remote(mid_b.at[(z + d) % NZ], last_b.at[z], along_z(d)) for d in range(1, NZ)])
    sent += red_a2 + red_b2
    last_a[x] = mid_a[x]
    last_b[z] = mid_b[z]

    keep_a[0].wait()
    arrive(ret_a1)
    others = [(d, k) for d in range(NZ) for k in range(NC) if d or k]
    ret_a2 = start([remote(ret_a.at[(z + d) % NZ, (c + k) % NC], back.at[0, z, c], along_z(d, k)) for d, k in others])
    keep_b[0].wait()
    arrive(ret_b1)
    ret_b2 = start([remote(ret_b.at[(x + d) % NX, (c + k) % NC], back.at[1, x, c], along_x(d, k)) for d, k in others])
    sent += ret_a2 + ret_b2
    stay = start([here(ret_a.at[z, c], back.at[0, z, c]), here(ret_b.at[x, c], back.at[1, x, c])])

    @pl.when(at_end)
    def _():
        end_tiles.wait()

    @pl.when(clip < 3)
    def _():
        move_tiles.wait_recv()

    def serve(n, carry):
        fetch[n // TILES, (n // (NZ * NC)) % NX, (n // NC) % NZ, n % NC] = tiles[served_ref[n]]
        return carry

    lax.fori_loop(0, SLOTS, serve, 0)
    keep_fa = start([here(fetch.at[0, x], get_a.at[:, :, x])])
    keep_fb = start([here(fetch.at[1, z], get_b.at[:, :, z])])
    get_a1 = start([remote(fetch.at[0, (x + d) % NX], get_a.at[:, :, x], along_x(d)) for d in range(1, NX)])
    get_b1 = start([remote(fetch.at[1, (z + d) % NZ], get_b.at[:, :, z], along_z(d)) for d in range(1, NZ)])
    sent += get_a1 + get_b1

    arrive(pool_a2)
    arrive(pool_b2)
    pool_3 = start([remote(every.at[c], every.at[c], along_x(0, 1))])
    sent += pool_3

    arrive(red_a2)
    arrive(red_b2)
    for b in range(BLK):
        coarse[b, top] = total(last_a, (b,)).astype(BF16)
        coarse[b, bottom] = total(last_b, (b,)).astype(BF16)
    put_coarse = start([here(coarse, coarse_ref)])

    keep_fa[0].wait()
    arrive(get_a1)
    get_a2 = start([remote(get_a.at[(z + d) % NZ, (c + k) % NC], got.at[0, z, c], along_z(d, k)) for d, k in others])
    keep_fb[0].wait()
    arrive(get_b1)
    get_b2 = start([remote(get_b.at[(x + d) % NX, (c + k) % NC], got.at[1, x, c], along_x(d, k)) for d, k in others])
    sent += get_a2 + get_b2
    stay += start([here(get_a.at[z, c], got.at[0, z, c]), here(get_b.at[x, c], got.at[1, x, c])])

    arrive(ret_a2)
    arrive(ret_b2)
    arrive(pool_3)
    arrive(get_a2)
    arrive(get_b2)
    for copy in stay + put_coarse:
        copy.wait()
    for copy in sent:
        copy.wait_send()

    @pl.when(clip > 0)
    def _():
        move_pool.wait_send()
        move_tiles.wait_send()


def exchange(served, pick_a, pick_b, frames, tail, ret, terms, pooled):
    smem = pl.BlockSpec(memory_space=pltpu.SMEM)
    hbm = pl.BlockSpec(memory_space=pl.ANY)
    tile = (PIX, PIX)
    shape = lambda *s: jax.ShapeDtypeStruct(s + tile, BF16)
    half = lambda *s: pltpu.VMEM(s + (HALF, PIX), BF16)
    full = lambda *s: pltpu.VMEM(s + tile, BF16)
    outs = pl.pallas_call(
        exchange_kernel,
        in_specs=[smem] * 3 + [hbm] * 5,
        out_specs=[hbm] * 8,
        out_shape=[
            shape(2, 4, NC, 4), shape(2, 4, NC, 4), shape(NC, NX, NZ, BLK), shape(BLK),
            shape(NZ, NC, NX), shape(NX, NC, NZ), shape(NZ, NC, NX), shape(NX, NC, NZ),
        ],
        scratch_shapes=[
            full(TILES), full(2, 4, 4, NC), full(TILES + 1), full(2, NX, NZ, BLK),
            full(NX, NZ, BLK), full(BLK),
            half(NZ, NX, BLK), half(NX, NZ, BLK), half(NX, BLK), half(NZ, BLK),
            half(NX, BLK), half(NZ, BLK), full(BLK),
            pltpu.SemaphoreType.DMA((80,)), pltpu.SemaphoreType.DMA((80,)),
            pltpu.SemaphoreType.DMA((16,)),
        ],
        compiler_params=pltpu.CompilerParams(
            collective_id=0, has_side_effects=True, vmem_limit_bytes=56 * 2**20),
        name="exchange",
    )(served, pick_a, pick_b, frames, tail, ret.reshape(2, 4, 4, NC, PIX, PIX), terms, pooled)
    return outs[:4]


def finish_kernel(
    slot_ref, ctile_ref, first_ref, order_ref, perm_ref, widen_ref,
    fine_ref, coarse_ref, got_ref, every_ref, back_ref, csum_ref,
    grad_a, grad_b, raw
):
    step = pl.program_id(0)
    scale = 1.0 / 16.0
    flip = (((0,), (0,)), ((), ()))

    @pl.when(step == 0)
    def _():
        for b in range(BLK):
            raw[b] = lax.dot_general(perm_ref[...], csum_ref[b], flip, preferred_element_type=F32).astype(BF16)

    fine = lax.dot_general(fine_ref[0], got_ref[0], flip, preferred_element_type=F32) * scale
    coarse = lax.dot_general(coarse_ref[0], every_ref[0], flip, preferred_element_type=F32) * scale
    grad_a[0] = (fine.astype(BF16).astype(F32) + coarse).astype(BF16)

    rows = pl.ds(pl.multiple_of((step % 16) * SIDE, SIDE), SIDE)
    spread = dot(widen_ref[...], raw[step // 16, rows, :]) * scale

    def add(n, value):
        return value + back_ref[order_ref[n]].astype(F32)

    grad_b[0] = lax.fori_loop(first_ref[step], first_ref[step + 1], add, spread).astype(BF16)


def finish(slots, ctile, first, order, fine, coarse, got, every, back, csum):
    one = (1, PIX, PIX)
    tile = lambda q, *s: (q, 0, 0)
    whole = lambda q, *s: (0, 0)
    out = jax.ShapeDtypeStruct((TILES, PIX, PIX), BF16)
    return pl.pallas_call(
        finish_kernel,
        grid_spec=pltpu.PrefetchScalarGridSpec(
            num_scalar_prefetch=4,
            grid=(TILES,),
            in_specs=[
                pl.BlockSpec((PIX, PIX), whole),
                pl.BlockSpec((PIX, SIDE), whole),
                pl.BlockSpec(one, tile),
                pl.BlockSpec(one, tile),
                pl.BlockSpec(one, lambda q, s, ct, f, o: (s[q], 0, 0)),
                pl.BlockSpec(one, lambda q, s, ct, f, o: (ct[q], 0, 0)),
                pl.BlockSpec((SLOTS, PIX, PIX), lambda q, *s: (0, 0, 0), pipeline_mode=pl.Buffered(1)),
                pl.BlockSpec((BLK, PIX, PIX), lambda q, *s: (0, 0, 0)),
            ],
            out_specs=[pl.BlockSpec(one, tile), pl.BlockSpec(one, tile)],
            scratch_shapes=[pltpu.VMEM((BLK, PIX, PIX), BF16)],
        ),
        out_shape=[out, out],
        compiler_params=pltpu.CompilerParams(vmem_limit_bytes=40 * 2**20),
        name="finish",
    )(slots, ctile, first, order, jnp.asarray(block_rows(), BF16),
      jnp.asarray(pool_rows().T, BF16), fine, coarse, got, every, back, csum)


def plan(owner, local, c_owner, c_block, me):
    ids = np.arange(TILES)
    xs, zs, cs = ids // (NZ * NC), (ids // NC) % NZ, ids % NC
    before = jnp.asarray(ids[None, :] < ids[:, None])
    mine = lax.dynamic_slice_in_dim(owner, me * TILES, TILES)
    rank = jnp.sum((mine[:, None] == mine[None, :]) & before, axis=1)
    ox, oz, oc = mine // (NZ * NC), (mine // NC) % NZ, mine % NC
    ret_slot = jnp.where(rank == 0, mine, TILES + (oz * NX + ox) * NC + oc)
    got_slot = jnp.where(rank == 0, (oz * NC + oc) * NX + ox, TILES + (ox * NC + oc) * NZ + oz)
    hit = (owner == me).reshape(TILES, TILES)
    ordinal = jnp.sum(hit[:, None, :] & before[None], axis=2)
    local = local.reshape(TILES, TILES)
    asked, valid = [], []
    for k in range(2):
        chosen = hit & (ordinal == k)
        asked.append(jnp.sum(jnp.where(chosen, local, 0), axis=1))
        valid.append(jnp.any(chosen, axis=1))
    order_b = (ids.reshape(NX, NZ, NC).transpose(1, 0, 2)).reshape(-1)
    served = jnp.concatenate([asked[0], asked[1][order_b]])
    back_a = (ids.reshape(NX, NZ, NC).transpose(1, 2, 0)).reshape(-1)
    back_b = (ids.reshape(NX, NZ, NC).transpose(0, 2, 1)).reshape(-1)
    key = jnp.concatenate([
        jnp.where(valid[0], asked[0], TILES)[back_a],
        jnp.where(valid[1], asked[1], TILES)[back_b],
    ])
    spot = jnp.arange(SLOTS)
    place = jnp.sum((key[None, :] < key[:, None]) | ((key[None, :] == key[:, None]) & (spot[None, :] < spot[:, None])), axis=1)
    order = jnp.sum(jnp.where(place[None, :] == spot[:, None], spot[None, :], 0), axis=1)
    first = jnp.sum(key[None, :] < jnp.arange(TILES + 1)[:, None], axis=1)
    c_mine = lax.dynamic_slice_in_dim(c_owner, me * TILES, TILES)
    b_mine = lax.dynamic_slice_in_dim(c_block, me * TILES, TILES)
    ctile = ((c_mine % NC) * (NX * NZ) + c_mine // NC) * BLK + b_mine
    c_hit = spot[:, None] == ctile[None, :]
    pick_a = jnp.min(jnp.where(c_hit, ids[None, :], TILES), axis=1)
    pick_b = jnp.max(jnp.where(c_hit, ids[None, :], -1), axis=1)
    pick_b = jnp.where((pick_b == pick_a) | (pick_b < 0), TILES, pick_b)
    as_int = lambda v: v.astype(jnp.int32)
    return tuple(map(as_int, (ret_slot, got_slot, served, order, first, ctile, pick_a, pick_b)))


def body(frames, tail, cotangent, window_base, window_frac, fine_owner, fine_local, coarse_owner, coarse_block):
    frames = frames[0]
    me = lax.axis_index("space")
    ret_slot, got_slot, served, order, first, ctile, pick_a, pick_b = plan(
        fine_owner[0, :, 0], fine_local[0], coarse_owner[0, :, 0], coarse_block[0], me)
    fine, coarse, ret, terms, pooled = prep(
        ret_slot, cotangent[0], window_base[0], window_frac[0], frames, tail)
    got, back, every, csum = exchange(served, pick_a, pick_b, frames, tail, ret, terms, pooled)
    flat = lambda v: v.reshape(-1, PIX, PIX)
    grad_a, grad_b = finish(got_slot, ctile, first, order, fine, coarse, flat(got), flat(every), flat(back), csum)
    return grad_a[None], grad_b[None]


def solution(mesh):
    in_specs = (
        P("clip", "space", None, None),
        P("space", None, None),
        P("clip", "space", None, None, None),
        P("clip", "space", None, None, None),
        P("clip", "space", None, None, None),
        P("clip", None, None),
        P("clip", None),
        P("clip", None, None),
        P("clip", None),
    )
    out_specs = (P("clip", "space", None, None), P("clip", "space", None, None))
    return jax.shard_map(body, mesh=mesh, in_specs=in_specs, out_specs=out_specs, check_vma=False)
```

time: 514 us -> 333 us (0.65)
  the two profiles are of different devices: /device:TPU:56 before, /device:TPU:1 now
where the time goes in v1:
time: 333 us; the launch traced here: 331 us
  Pallas kernels  308 us (92%)
  local copies, waits for them, and re-layouts  11.6 us (3%)
  other arithmetic  10.7 us (3%)
    pallas_call x1, Pallas kernels, exchange(): pl.pallas_call(exchange_kernel, in_specs=[smem] * 3 + [hbm] * 5, out_spec...  251 us
    pallas_call x1, Pallas kernels, prep(): pl.pallas_call(prep_kernel, grid_spec=pltpu.PrefetchScalarGridSpec(num_sc...  28.8 us
    pallas_call x1, Pallas kernels, finish(): pl.pallas_call(finish_kernel, grid_spec=pltpu.PrefetchScalarGridSpec(num_...  28.4 us
    unnamed x24, local copies, waits for them, and re-layouts  8.67 us

profile of v1, /device:TPU:1, one launch (start us, length us, event | category | flops | bytes accessed | tf_op | source)
XLA Modules:
  0.0 330.9 jit_solution(5297594878207288396)
XLA Ops:
  0.7 0.9 add_bitcast_fusion
  1.6 0.7 compare_reduce_fusion
  2.3 0.7 fusion.4
  3.0 0.9 convert_reduce_fusion.3
  4.0 0.8 compare_select_fusion.8
  4.8 0.7 compare_select_fusion.9.slot_ref
  6.1 1.3 reduce.5
  7.4 0.7 pad_clamp_fusion.2
  8.1 0.7 pad_clamp_fusion.1
  8.8 0.7 pad_clamp_fusion
  9.5 1.3 convert_reduce_fusion
  11.1 0.7 gather_fusion.2
  11.9 0.7 gather_fusion.1
  12.6 0.7 pad_add_fusion.1.served_ref
  13.2 0.7 gather_fusion
  13.9 0.6 or_select_fusion
  14.9 2.2 copy.29
  17.1 28.8 %prep.1 = (bf16[32,256,256]{2,1,0:T(8,128)(2,1)S(1)}, bf16[32,256,256]{2,1,0:T(8,128)(2,1)S(1)}, bf16[64,256,256]{2,1,0:T(8,128)(2,1)}, bf16[32,256,256]{2,1,0:T(8,128)(2,1)}, bf16[2,2,256,256]{3,2,1,0:T(8,128)(2,1)S(1)}) custom-call(s32[32]{0:T(128)S(1)} %get-tuple-element.28.slot_ref, bf16[288,81]{1,0:T(8,128)(2,1)S(1)} %copy-done.6, ...), custom_call_target="tpu_custom_call" | custom-call | tf_op jit(solution)/shard_map/prep/pallas_call | solution.py:124
  46.0 2.0 copy-done
  48.0 0.8 copy-done.3
  48.8 250.5 %exchange.1 = (bf16[2,4,2,4,256,256]{5,4,3,2,1,0:T(8,128)(2,1)}, bf16[2,4,2,4,256,256]{5,4,3,2,1,0:T(8,128)(2,1)}, bf16[2,4,4,2,256,256]{5,4,3,2,1,0:T(8,128)(2,...) custom-call(s32[64]{0:T(128)} %pad_add_fusion.1.served_ref, ...), custom_call_target="tpu_custom_call" | custom-call | tf_op jit(solution)/shard_map/exchange/pallas_call | solution.py:388
  299.3 2.2 copy-done.1
  301.5 0.9 copy-done.4
  302.5 28.4 %finish.1 = (bf16[32,256,256]{2,1,0:T(8,128)(2,1)}, bf16[32,256,256]{2,1,0:T(8,128)(2,1)}) custom-call(s32[32]{0:T(128)S(1)} %compare_select_fusion.9.slot_ref, s32[32]{0:T(128)S(1)} %get-tuple-element.36.ctile_ref, s32[33]{0:T(128)S(1)} %convert_reduce_fusion.2.first_ref, s32[64]{0:T(128)S(1)} %select_reduce_fusion.order_ref, ...), custom_call_target="tpu_custom_call" | custom-call | tf_op jit(solution)/shard_map/finish/pallas_call | solution.py:443
  (30 shorter events, 1.6 us)
Async XLA Ops:
  0.6 16.5 %copy-start.2 = (bf16[256,256]{1,0:T(8,128)(2,1)S(1)}, bf16[256,256]{1,0:T(8,128)(2,1)}, u32[]{:S(2)}) copy-start(bf16[256,256]{1,0:T(8,128)(2,1)} %constant.117.clone.perm_ref) | copy-start | bytes 393220
  0.6 16.5 %copy-start.9 = (bf16[16,256]{1,0:T(8,128)(2,1)S(1)}, bf16[16,256]{1,0:T(8,128)(2,1)}, u32[]{:S(2)}) copy-start(bf16[16,256]{1,0:T(8,128)(2,1)} %constant.116.clone.pool_ref) | copy-start | bytes 24580
  0.7 16.5 %copy-start.6 = (bf16[288,81]{1,0:T(8,128)(2,1)S(1)}, bf16[288,81]{1,0:T(8,128)(2,1)}, u32[]{:S(2)}) copy-start(bf16[288,81]{1,0:T(8,128)(2,1)} %constant.115.clone.spread_ref) | copy-start | bytes 139972
  0.7 16.5 %copy-start.7 = (bf16[1,32,2,2,256]{4,3,2,1,0:T(2,128)(2,1)S(1)}, bf16[1,32,2,2,256]{4,3,2,1,0:T(2,128)(2,1)}, u32[]{:S(2)}) copy-start(bf16[1,32,2,2,256]{4,3,2,1,0:T(2,128)(2,1)} %param.27) | copy-start | bytes 196612
  0.7 16.5 %copy-start.5 = (s32[1,32,2,2,256]{4,3,2,1,0:T(2,128)S(1)}, s32[1,32,2,2,256]{4,3,2,1,0:T(2,128)}, u32[]{:S(2)}) copy-start(s32[1,32,2,2,256]{4,3,2,1,0:T(2,128)} %param.26) | copy-start | bytes 393220
  4.0 42.0 %copy-start.10 = (s32[64]{0:T(128)}, s32[64]{0:T(128)S(1)}, u32[]{:S(2)}) copy-start(s32[64]{0:T(128)S(1)} %get-tuple-element.27.pick_a) | copy-start | bytes 772
  46.0 2.0 copy-start
  48.0 0.8 copy-start.3
  48.8 250.5 %copy-start.8 = (bf16[256,16]{1,0:T(8,128)(2,1)S(1)}, bf16[256,16]{1,0:T(8,128)(2,1)}, u32[]{:S(2)}) copy-start(bf16[256,16]{1,0:T(8,128)(2,1)} %constant.118.clone.widen_ref) | copy-start | bytes 24580
  299.3 2.2 copy-start.1
  301.5 0.9 copy-start.4

commit v2 on v1

v2 whole, which is shorter than its diff:
```python
import functools

import jax
import jax.numpy as jnp
import numpy as np
from jax import lax
from jax.experimental import pallas as pl
from jax.experimental.pallas import tpu as pltpu
from jax.sharding import PartitionSpec as P

MESH = pl.DeviceIdType.MESH
POOL = 4
SIDE = 16
WIN = 9
PIX = 256
HALF = PIX // 2
NX, NZ, NC = 4, 4, 2
BLK = 2
TILES = 32
SLOTS = 2 * TILES
F32 = jnp.float32
BF16 = jnp.bfloat16


def placement():
    spread = np.zeros((2 * WIN * SIDE, WIN * WIN), np.float32)
    for a in range(WIN):
        for k in range(WIN):
            spread[a * SIDE + k, a * WIN + k] = 1
            spread[WIN * SIDE + a * SIDE + k + 1, a * WIN + k] = 1
    return spread


def pool_rows():
    rows = np.zeros((SIDE, PIX), np.float32)
    for y in range(SIDE):
        for x in range(SIDE):
            rows[(y // POOL) * POOL + x // POOL, y * SIDE + x] = 1
    return rows


def block_rows():
    rows = np.zeros((PIX, PIX), np.float32)
    for ty in range(4):
        for tx in range(4):
            for a in range(4):
                for b in range(4):
                    rows[(ty * 4 + a) * 16 + tx * 4 + b, (ty * 4 + tx) * 16 + a * 4 + b] = 1
    return rows


def dot(a, b):
    return jnp.dot(a, b, preferred_element_type=F32)


def window_map(spread, cot, base, frac):
    placed = dot(spread, cot)
    rows = WIN * SIDE
    fx = frac[0:1].astype(F32)
    fy = frac[1:2].astype(F32)
    shape = (SIDE, PIX)
    ox = jnp.broadcast_to(base[0:1] - WIN // 2, shape)
    oy = jnp.broadcast_to(base[1:2] - WIN // 2, shape)
    across = (1.0 - fx) * placed[:rows] + fx * placed[rows:]
    groups = []
    for y in range(WIN + 1):
        value = None
        if y < WIN:
            value = (1.0 - fy) * across[y * SIDE : (y + 1) * SIDE]
        if y > 0:
            below = fy * across[(y - 1) * SIDE : y * SIDE]
            value = below if value is None else value + below
        groups.append(value)
    for step in (1, 2, 4):
        chosen = (ox & step) != 0
        groups = [jnp.where(chosen, pltpu.roll(g, step, 0), g) for g in groups]
    zero = jnp.zeros(shape, F32)
    for step in (1, 2, 4):
        chosen = (oy & step) != 0
        count = min(SIDE, len(groups) + step)
        groups = [
            jnp.where(
                chosen,
                groups[y - step] if y >= step else zero,
                groups[y] if y < len(groups) else zero,
            )
            for y in range(count)
        ]
    return jnp.concatenate(groups, axis=0).astype(BF16)


def plan_kernel(owner_ref, local_ref, c_owner_ref, c_block_ref, out_ref):
    me = lax.axis_index("space")
    total = functools.partial(jnp.sum, keepdims=True)
    sub, lane = (lax.broadcasted_iota(jnp.int32, (TILES, TILES), n) for n in range(2))
    wide_sub, wide_lane = (lax.broadcasted_iota(jnp.int32, (TILES, SLOTS), n) for n in range(2))
    tall_sub, tall_lane = (lax.broadcasted_iota(jnp.int32, (SLOTS, TILES), n) for n in range(2))
    slot_sub, slot_lane = (lax.broadcasted_iota(jnp.int32, (SLOTS, SLOTS), n) for n in range(2))
    one = (sub == lane).astype(F32)
    row_of = lambda n: lax.broadcasted_iota(jnp.int32, (TILES, 128), n)
    per_row = 128 // TILES
    pick_row = (lax.broadcasted_iota(jnp.int32, (TILES, 8), 0) // per_row == lax.broadcasted_iota(jnp.int32, (TILES, 8), 1)).astype(F32)
    in_part = row_of(0) % per_row == row_of(1) // TILES
    fold = (lax.broadcasted_iota(jnp.int32, (128, TILES), 0) % TILES == lax.broadcasted_iota(jnp.int32, (128, TILES), 1)).astype(F32)

    def square(ref):
        rows = dot(pick_row, ref[...].astype(F32))
        return dot(jnp.where(in_part, rows, 0.0), fold).astype(jnp.int32)

    owner, local, c_owner, c_block = (square(r) for r in (owner_ref, local_ref, c_owner_ref, c_block_ref))
    flip = (((0,), (0,)), ((), ()))

    def turned(v):
        return lax.dot_general(v.astype(F32), one, flip, preferred_element_type=F32).astype(jnp.int32)

    def mine(v):
        row = total(jnp.where(sub == me, v, 0), axis=0)
        return row, total(jnp.where(lane == me, turned(v), 0), axis=1)

    def parts(v):
        return v // (NZ * NC), (v // NC) % NZ, v % NC

    own_row, own_col = mine(owner)
    same = own_row == own_col
    rank_row = total(jnp.where(same & (sub < lane), 1, 0), axis=0)
    rank_col = total(jnp.where(same & (lane < sub), 1, 0), axis=1)
    ox, oz, oc = parts(own_row)
    got_slot = jnp.where(rank_row == 0, (oz * NC + oc) * NX + ox, TILES + (ox * NC + oc) * NZ + oz)
    ox, oz, oc = parts(own_col)
    ret_slot = jnp.where(rank_col == 0, own_col, TILES + (oz * NX + ox) * NC + oc)
    filled = total(jnp.where(ret_slot == wide_lane, wide_sub, 0), axis=0)

    ctile_row, ctile_col = (
        ((o % NC) * (NX * NZ) + o // NC) * BLK + b for o, b in zip(mine(c_owner), mine(c_block)))
    named = ctile_col == wide_lane
    pick_a = jnp.min(jnp.where(named, wide_sub, TILES), axis=0, keepdims=True)
    pick_b = jnp.max(jnp.where(named, wide_sub, -1), axis=0, keepdims=True)
    pick_b = jnp.where((pick_b == pick_a) | (pick_b < 0), TILES, pick_b)

    def asked(hit, ids, earlier, axis):
        seen = hit.astype(F32)
        before = dot(earlier, seen) if axis == 0 else dot(seen, earlier)
        out = []
        for k in range(2):
            chosen = hit & (before.astype(jnp.int32) == k)
            value = total(jnp.where(chosen, ids, 0), axis=axis)
            count = total(jnp.where(chosen, 1, 0), axis=axis)
            out.append((value, jnp.where(count > 0, value, TILES)))
        return out

    (_, key0_row), (_, key1_row) = asked(turned(owner) == me, turned(local), (lane < sub).astype(F32), 0)
    (ask0, key0), (ask1, key1) = asked(owner == me, local, (sub < lane).astype(F32), 1)
    px, pz, pc = parts(wide_sub)
    served = total(jnp.where(wide_lane == wide_sub, ask0, 0), axis=0)
    served += total(jnp.where(wide_lane == TILES + (pz * NX + px) * NC + pc, ask1, 0), axis=0)
    key_row = total(jnp.where(wide_lane == (pz * NC + pc) * NX + px, key0, 0), axis=0)
    key_row += total(jnp.where(wide_lane == TILES + (px * NC + pc) * NZ + pz, key1, 0), axis=0)
    px, pz, pc = parts(tall_lane)
    key_col = total(jnp.where(tall_sub == (pz * NC + pc) * NX + px, key0_row, 0), axis=1)
    key_col += total(jnp.where(tall_sub == TILES + (px * NC + pc) * NZ + pz, key1_row, 0), axis=1)
    ahead = (key_row < key_col) | ((key_row == key_col) & (slot_lane < slot_sub))
    place = total(jnp.where(ahead, 1, 0), axis=1)
    order = total(jnp.where(place == slot_lane, slot_sub, 0), axis=0)
    first = total(jnp.where(key_col < slot_lane, 1, 0), axis=0)
    out_ref[...] = jnp.zeros((8, SLOTS), jnp.int32)
    for row, value in enumerate((served, filled, pick_a, pick_b, ctile_row, got_slot, order, first)):
        out_ref[row : row + 1, : value.shape[1]] = value


SERVED, FILLED, PICK_A, PICK_B, CTILE, GOT, ORDER, FIRST = range(8)


def plan(*ids):
    vmem = pl.BlockSpec(memory_space=pltpu.VMEM)
    return pl.pallas_call(
        plan_kernel, in_specs=[vmem] * 4, out_specs=vmem,
        out_shape=jax.ShapeDtypeStruct((8, SLOTS), jnp.int32), name="plan",
    )(*ids)


def exchange_kernel(
    table, spread_ref, pool_ref, perm_ref, widen_ref, base, frac, frames, tail, cot_ref,
    got, grad_ref, maps_ref, query_ref, back, below_every, every, ret_a, ret_b, get_a, get_b,
    first, cot, tiles, fine, other, terms, slots, partial, sibling, raw, pown,
    up_a, down_a, up_b, down_b, red_a, red_b, mid_a, mid_b, last_a, last_b, coarse, running,
    send, recv, local
):
    scale = 1.0 / 16.0
    clip = lax.axis_index("clip")
    space = lax.axis_index("space")
    x = space // (NZ * NC)
    z = (space // NC) % NZ
    c = space % NC
    counts = {"remote": 0, "local": 0}

    def along_x(d, core=0):
        return (clip, (((x + d) % NX) * NZ + z) * NC + (c + core) % NC)

    def along_z(d, core=0):
        return (clip, (x * NZ + (z + d) % NZ) * NC + (c + core) % NC)

    def remote(src, dst, device):
        n = counts["remote"]
        counts["remote"] += 1
        return pltpu.make_async_remote_copy(
            src_ref=src, dst_ref=dst, send_sem=send.at[n], recv_sem=recv.at[n],
            device_id=device, device_id_type=MESH)

    def here(src, dst):
        n = counts["local"]
        counts["local"] += 1
        return pltpu.make_async_copy(src, dst, local.at[n])

    def start(copies):
        for copy in copies:
            copy.start()
        return copies

    def arrive(copies):
        for copy in copies:
            copy.wait_recv()

    load = start([here(frames, first.at[pl.ds(0, TILES)]), here(cot_ref, cot)])
    at_end = clip == 3
    below = ((clip + 3) % 4, space)
    move_tiles = remote(frames, tiles, below)
    end_tiles = here(tail, tiles)
    pool_tail = here(tail, slots.at[pl.ds(0, TILES)])

    @pl.when(at_end)
    def _():
        end_tiles.start()

    @pl.when(clip == 0)
    def _():
        pool_tail.start()

    barrier = pltpu.get_barrier_semaphore()
    greeted = [along_x(d, k) for d in range(1, NX) for k in range(NC)]
    greeted += [along_z(d, k) for d in range(1, NZ) for k in range(NC)]
    greeted += [along_x(0, 1), ((clip + 1) % 4, space)]
    for device in greeted:
        pl.semaphore_signal(barrier, inc=1, device_id=device, device_id_type=MESH)
    pl.semaphore_wait(barrier, len(greeted))

    sent = []

    def pool(source, target):
        def one(n, carry):
            rows = pl.ds(pl.multiple_of((n % 16) * SIDE, SIDE), SIDE)
            raw[n // 16, rows, :] = (dot(pool_ref[...], source[n]) * scale).astype(BF16)
            return carry
        lax.fori_loop(0, TILES, one, 0)
        for b in range(BLK):
            target[b] = dot(perm_ref[...], raw[b]).astype(BF16)

    @pl.when(clip > 0)
    def _():
        move_tiles.start()

    load[0].wait()

    @pl.when(clip > 0)
    def _():
        pool(first, pown)

    @pl.when(clip == 0)
    def _():
        pool_tail.wait()
        pool(slots, pown)

    top, bottom = pl.ds(0, HALF), pl.ds(HALF, HALF)
    keep_pool = start([here(pown, every.at[c, x, z])])
    pool_a1 = start([remote(pown.at[:, top], every.at[c, x, z, :, top], along_x(d)) for d in range(1, NX)])
    pool_b1 = start([remote(pown.at[:, bottom], every.at[c, x, z, :, bottom], along_z(d)) for d in range(1, NZ)])
    sent += pool_a1 + pool_b1

    def products(begin, end, level, keep, put):
        def one(n, carry):
            for q in (2 * n, 2 * n + 1):
                weights = window_map(spread_ref[...], cot[q, level], base[q, level], frac[q, level])
                put[q] = (dot(weights, first[q]) * scale).astype(BF16)
                keep[q] = weights.T
            return carry
        lax.fori_loop(begin // 2, end // 2, one, 0)

    load[1].wait()
    products(0, TILES // 2, 0, fine, terms)

    keep_pool[0].wait()
    arrive(pool_a1)
    line = every.at[c, :, z, :, top]
    pool_a2 = start([remote(line, line, along_z(d)) for d in (1, NZ - 1)])
    arrive(pool_b1)
    line = every.at[c, x, :, :, bottom]
    pool_b2 = start([remote(line, line, along_x(d)) for d in (1, NX - 1)])
    sent += pool_a2 + pool_b2

    products(TILES // 2, TILES, 0, fine, terms)
    put_maps = start([here(fine, maps_ref)])

    def fill_slots(half, source, row):
        def one(n, carry):
            slots[half * TILES + n] = source[table[row, half * TILES + n]]
            return carry
        lax.fori_loop(0, TILES, one, 0)

    def group(half, n):
        return slots.at[pl.ds(half * TILES + n * 8, 8)]

    def first_hop(source, row, into_a, into_b):
        fill_slots(0, source, row)
        stay_a = start([here(group(0, x), into_a.at[:, x])])
        hop_a = start([remote(group(0, (x + d) % NX), into_a.at[:, x], along_x(d)) for d in range(1, NX)])
        fill_slots(1, source, row)
        stay_b = start([here(group(1, z), into_b.at[:, z])])
        hop_b = start([remote(group(1, (z + d) % NZ), into_b.at[:, z], along_z(d)) for d in range(1, NZ)])
        return stay_a, hop_a, stay_b, hop_b

    others = [(d, k) for d in range(NZ) for k in range(NC) if d or k]

    def second_hop(hops, from_a, from_b, into):
        stay_a, hop_a, stay_b, hop_b = hops
        into_a = into.at[pl.ds((z * NC + c) * 4, 4)]
        into_b = into.at[pl.ds(TILES + (x * NC + c) * 4, 4)]
        stay_a[0].wait()
        arrive(hop_a)
        far = start([remote(from_a.at[(z + d) % NZ * NC + (c + k) % NC], into_a, along_z(d, k)) for d, k in others])
        near = start([here(from_a.at[z * NC + c], into_a)])
        stay_b[0].wait()
        arrive(hop_b)
        far += start([remote(from_b.at[(x + d) % NX * NC + (c + k) % NC], into_b, along_x(d, k)) for d, k in others])
        near += start([here(from_b.at[x * NC + c], into_b)])
        return far, near

    ret_hops = first_hop(terms, FILLED, ret_a, ret_b)

    products(0, TILES // 2, 1, other, first)

    x_up, x_down, z_up, z_down = (x + 1) % NX, (x + NX - 1) % NX, (z + 1) % NZ, (z + NZ - 1) % NZ
    low, high = pl.ds(0, 2), pl.ds(2, 2)
    arrive(pool_a2)
    line_up, line_down = every.at[c, low, z_down, :, top], every.at[c, high, z_up, :, top]
    pool_a3 = start([remote(line_up, line_up, along_z(1)), remote(line_down, line_down, along_z(NZ - 1))])
    arrive(pool_b2)
    line_up, line_down = every.at[c, x_down, low, :, bottom], every.at[c, x_up, high, :, bottom]
    pool_b3 = start([remote(line_up, line_up, along_x(1)), remote(line_down, line_down, along_x(NX - 1))])
    sent += pool_a3 + pool_b3

    products(TILES // 2, TILES, 1, other, first)
    first[TILES] = jnp.zeros((PIX, PIX), BF16)

    def fill(which, core):
        def one(n, carry):
            value = first[table[PICK_A, core * TILES + n]].astype(F32)
            value = value + first[table[PICK_B, core * TILES + n]].astype(F32)
            partial[which, n // (NZ * BLK), (n // BLK) % NZ, n % BLK] = value.astype(BF16)
            return carry
        lax.fori_loop(0, TILES, one, 0)

    fill(1, 1 - c)
    share = start([remote(partial.at[1], sibling, along_x(0, 1))])
    fill(0, c)
    arrive(share)

    def join(n, carry):
        at = (n // (NZ * BLK), (n // BLK) % NZ, n % BLK)
        mine = partial[(0, *at)].astype(F32)
        partial[(0, *at)] = (mine + sibling[at].astype(F32)).astype(BF16)
        return carry

    lax.fori_loop(0, TILES, join, 0)

    mine = partial.at[0]
    z_far, x_far = (z + 2) % NZ, (x + 2) % NX
    red_1 = start([
        remote(mine.at[low, z_far, :, top], up_a, along_z(1)),
        remote(mine.at[high, z_far, :, top], down_a, along_z(NZ - 1)),
        remote(mine.at[x_far, low, :, bottom], up_b, along_x(1)),
        remote(mine.at[x_far, high, :, bottom], down_b, along_x(NX - 1)),
    ])
    arrive(red_1)

    def pass_on(n, carry):
        i, b = n // BLK, n % BLK
        for at, extra in (
            ((0, i, z_up, b, top), up_a), ((0, i + 2, z_down, b, top), down_a),
            ((0, x_up, i, b, bottom), up_b), ((0, x_down, i + 2, b, bottom), down_b),
        ):
            partial[at] = (partial[at].astype(F32) + extra[i, b].astype(F32)).astype(BF16)
        return carry

    lax.fori_loop(0, 2 * BLK, pass_on, 0)
    red_2 = start([
        remote(mine.at[:, z_up, :, top], red_a.at[0], along_z(1)),
        remote(mine.at[:, z_down, :, top], red_a.at[1], along_z(NZ - 1)),
        remote(mine.at[x_up, :, :, bottom], red_b.at[0], along_x(1)),
        remote(mine.at[x_down, :, :, bottom], red_b.at[1], along_x(NX - 1)),
    ])

    ret_far, stay = second_hop(ret_hops, ret_a, ret_b, back)
    sent += ret_far

    arrive(red_2)

    def middle(n, carry):
        i, b = n // BLK, n % BLK
        for at, extra, into in (((0, i, z, b, top), red_a, mid_a), ((0, x, i, b, bottom), red_b, mid_b)):
            value = partial[at].astype(F32) + extra[0, i, b].astype(F32) + extra[1, i, b].astype(F32)
            into[i, b] = value.astype(BF16)
        return carry

    lax.fori_loop(0, NX * BLK, middle, 0)
    red_a2 = start([remote(mid_a.at[(x + d) % NX], last_a.at[x], along_x(d)) for d in range(1, NX)])
    red_b2 = start([remote(mid_b.at[(z + d) % NZ], last_b.at[z], along_z(d)) for d in range(1, NZ)])
    sent += red_a2 + red_b2
    last_a[x] = mid_a[x]
    last_b[z] = mid_b[z]

    for copy in ret_hops[1] + ret_hops[3]:
        copy.wait_send()

    @pl.when(at_end)
    def _():
        end_tiles.wait()

    @pl.when(clip < 3)
    def _():
        move_tiles.wait_recv()

    get_hops = first_hop(tiles, SERVED, get_a, get_b)

    arrive(pool_a3)
    arrive(pool_b3)
    pool_4 = start([remote(every.at[c], below_every.at[c], below)])

    def total(buffer, at):
        value = buffer[(0, *at)].astype(F32)
        for n in range(1, 4):
            value = value + buffer[(n, *at)].astype(F32)
        return value

    arrive(red_a2)
    arrive(red_b2)
    for b in range(BLK):
        coarse[b, top] = total(last_a, (b,)).astype(BF16)
        coarse[b, bottom] = total(last_b, (b,)).astype(BF16)
    flip = (((0,), (0,)), ((), ()))
    for b in range(BLK):
        raw[b] = lax.dot_general(perm_ref[...], coarse[b], flip, preferred_element_type=F32).astype(BF16)

    get_far, near = second_hop(get_hops, get_a, get_b, got)
    sent += get_far
    stay += near

    arrive(pool_4)
    pool_5 = start([remote(below_every.at[c], below_every.at[c], along_x(0, 1))])
    sent += pool_4 + pool_5

    arrive(ret_far)
    for copy in get_hops[1] + get_hops[3]:
        copy.wait_send()
    for copy in stay:
        copy.wait()
    load_back = start([here(back, slots)])
    load_back[0].wait()
    for part in range(4):
        rows = pl.ds(part * 64, 64)
        running[0] = jnp.zeros((64, PIX), F32)

        def add(n, carry):
            running[n + 1] = running[n] + slots[table[ORDER, n], rows].astype(F32)
            return carry

        lax.fori_loop(0, SLOTS, add, 0)

        def gradient(n, carry):
            at = pl.ds(pl.multiple_of((n % 16) * SIDE, SIDE), SIDE)
            value = dot(widen_ref[rows], raw[n // 16, at]) * scale
            value = value + (running[table[FIRST, n + 1]] - running[table[FIRST, n]])
            terms[n, rows] = value.astype(BF16)
            return carry

        lax.fori_loop(0, TILES, gradient, 0)
    put = start([here(terms, grad_ref)])

    for copy in share + red_1 + red_2:
        copy.wait_send()
    arrive(pool_5)
    load_every = start([here(below_every, partial)])
    load_every[0].wait()

    def query(n, carry):
        at = table[CTILE, n]
        tile = partial[at // (NX * NZ * BLK), (at // (NZ * BLK)) % NX, (at // BLK) % NZ, at % BLK]
        other[n] = (dot(other[n], tile) * scale).astype(BF16)
        return carry

    lax.fori_loop(0, TILES, query, 0)
    put += start([here(other, query_ref)])

    arrive(get_far)
    for copy in put + put_maps:
        copy.wait()
    for copy in sent:
        copy.wait_send()

    @pl.when(clip > 0)
    def _():
        move_tiles.wait_send()


def exchange(table, frames, tail, cot, base, frac):
    smem = pl.BlockSpec(memory_space=pltpu.SMEM)
    vmem = pl.BlockSpec(memory_space=pltpu.VMEM)
    hbm = pl.BlockSpec(memory_space=pl.ANY)
    tile = (PIX, PIX)
    shape = lambda *s: jax.ShapeDtypeStruct(s + tile, BF16)
    half = lambda *s: pltpu.VMEM(s + (HALF, PIX), BF16)
    full = lambda *s: pltpu.VMEM(s + tile, BF16)
    outs = pl.pallas_call(
        exchange_kernel,
        in_specs=[smem] + [vmem] * 6 + [hbm] * 3,
        out_specs=[hbm] * 11,
        out_shape=[
            shape(SLOTS), shape(TILES), shape(TILES), shape(TILES), shape(SLOTS),
            shape(NC, NX, NZ, BLK), shape(NC, NX, NZ, BLK),
            shape(8, NX), shape(8, NZ), shape(8, NX), shape(8, NZ),
        ],
        scratch_shapes=[
            full(TILES + 1), pltpu.VMEM((TILES, 2, WIN * WIN, PIX), BF16),
            full(TILES), full(TILES), full(TILES), full(TILES),
            full(SLOTS), full(2, NX, NZ, BLK), full(NX, NZ, BLK),
            full(BLK), full(BLK),
            half(2, BLK), half(2, BLK), half(2, BLK), half(2, BLK),
            half(2, NX, BLK), half(2, NZ, BLK), half(NX, BLK), half(NZ, BLK),
            half(NX, BLK), half(NZ, BLK), full(BLK), pltpu.VMEM((SLOTS + 1, 64, PIX), F32),
            pltpu.SemaphoreType.DMA((80,)), pltpu.SemaphoreType.DMA((80,)),
            pltpu.SemaphoreType.DMA((24,)),
        ],
        compiler_params=pltpu.CompilerParams(
            collective_id=0, has_side_effects=True, vmem_limit_bytes=62 * 2**20),
        name="exchange",
    )(table, jnp.asarray(placement(), BF16), jnp.asarray(pool_rows(), BF16),
      jnp.asarray(block_rows(), BF16), jnp.asarray(pool_rows().T, BF16), base, frac, frames, tail, cot)
    return outs[:4]


GROUP = 4


def finish_kernel(table, maps_ref, query_ref, *refs):
    for n in range(GROUP):
        value = dot(maps_ref[n], refs[n][0]) * (1.0 / 16.0)
        refs[GROUP][n] = (value + query_ref[n].astype(F32)).astype(BF16)


def finish(table, maps, query, got):
    tile = lambda q, t: (q, 0, 0)
    block = pl.BlockSpec((GROUP, PIX, PIX), tile)
    return pl.pallas_call(
        finish_kernel,
        grid_spec=pltpu.PrefetchScalarGridSpec(
            num_scalar_prefetch=1,
            grid=(TILES // GROUP,),
            in_specs=[block, block] + [
                pl.BlockSpec((1, PIX, PIX), lambda q, t, n=n: (t[GOT, q * GROUP + n], 0, 0))
                for n in range(GROUP)
            ],
            out_specs=block,
        ),
        out_shape=jax.ShapeDtypeStruct((TILES, PIX, PIX), BF16),
        compiler_params=pltpu.CompilerParams(vmem_limit_bytes=60 * 2**20),
        name="finish",
    )(table, maps, query, *[got] * GROUP)


def body(frames, tail, cotangent, window_base, window_frac, fine_owner, fine_local, coarse_owner, coarse_block):
    table = plan(*(v.reshape(8, 128) for v in (fine_owner, fine_local, coarse_owner, coarse_block)))
    got, grad_b, maps, query = exchange(table, frames[0], tail, cotangent[0], window_base[0], window_frac[0])
    grad_a = finish(table, maps, query, got)
    return grad_a[None], grad_b[None]


def solution(mesh):
    in_specs = (
        P("clip", "space", None, None),
        P("space", None, None),
        P("clip", "space", None, None, None),
        P("clip", "space", None, None, None),
        P("clip", "space", None, None, None),
        P("clip", None, None),
        P("clip", None),
        P("clip", None, None),
        P("clip", None),
    )
    out_specs = (P("clip", "space", None, None), P("clip", "space", None, None))
    return jax.shard_map(body, mesh=mesh, in_specs=in_specs, out_specs=out_specs, check_vma=False)
```

time: 333 us -> 294 us (0.88)
  Pallas kernels: 308 us -> 282 us
  other arithmetic: 10.7 us -> 0 us
    pallas_call x1, Pallas kernels: 28.4 us -> 9.94 us  [finish(): pl.pallas_call(finish_kernel, grid_spec=pltpu.PrefetchScalarGridSpec(num_...]
    pallas_call x2, Pallas kernels: 279 us -> 272 us  [the longest x1 270 us: exchange(): pl.pallas_call(exchange_kernel, in_specs=[smem] + [vmem] * 6 + [hbm] * 3,...]
    unnamed x24 -> x2, local copies, waits for them, and re-layouts: 8.67 us -> 8.39 us
where the time goes in v2:
time: 294 us; the launch traced here: 291 us
  Pallas kernels  282 us (96%)
  local copies, waits for them, and re-layouts  8.39 us (3%)
    pallas_call x1, Pallas kernels, exchange(): pl.pallas_call(exchange_kernel, in_specs=[smem] + [vmem] * 6 + [hbm] * 3,...  270 us
    pallas_call x1, Pallas kernels, finish(): pl.pallas_call(finish_kernel, grid_spec=pltpu.PrefetchScalarGridSpec(num_...  9.94 us
    unnamed x2, local copies, waits for them, and re-layouts  8.39 us

profile of v2, /device:TPU:1, one launch (start us, length us, event | category | flops | bytes accessed | tf_op | source)
XLA Modules:
  0.0 290.9 jit_solution(1762775002613939393)
XLA Ops:
  0.6 2.1 plan.1.table
  2.8 3.8 %copy.17 = bf16[1,32,2,81,256]{4,3,2,1,0:T(8,128)(2,1)} copy(bf16[1,32,2,81,256]{4,2,3,1,0:T(2,128)(2,1)} %param.15) | data formatting | bytes 5308416 | tf_op args[2]
  6.5 269.8 %exchange.1 = (bf16[64,256,256]{2,1,0:T(8,128)(2,1)}, bf16[32,256,256]{2,1,0:T(8,128)(2,1)}, bf16[32,256,256]{2,1,0:T(8,128)(2,1)}, bf16[32,256,256]{2,1,0:T(8,1...) custom-call(s32[8,64]{1,0:T(8,128)} %plan.1.table, ...), custom_call_target="tpu_custom_call" | custom-call | tf_op jit(solution)/shard_map/exchange/pallas_call | solution.py:521
  276.3 9.9 %finish.1 = bf16[32,256,256]{2,1,0:T(8,128)(2,1)} custom-call(s32[8,64]{1,0:T(8,128)} %plan.1.table, bf16[32,256,256]{2,1,0:T(8,128)(2,1)} %get-tuple-element.6.maps_ref, bf16[32,256,256]{2,1,0:T(8,128)(2,1)} %get-tuple-element.7.query_ref, bf16[64,256,256]{2,1,0:T(8,128)(2,1)} %get-tuple-element.8.refs_0_.refs_1_.refs_2_.refs_3_, ...), custom_call_target="tpu_custom_call" | custom-call | tf_op jit(solution)/shard_map/finish/pallas_call | solution.py:561
  286.3 4.6 %copy.19 = bf16[1,32,256,256]{3,2,1,0:T(8,128)(2,1)} copy(bf16[1,32,256,256]{3,2,1,0:T(8,128)(2,1)} %bitcast.14) | data formatting | bytes 8388608

commit v3 on v2

--- a/solution.py
+++ b/solution.py
@@ -180,8 +180,8 @@
 
 def exchange_kernel(
     table, spread_ref, pool_ref, perm_ref, widen_ref, base, frac, frames, tail, cot_ref,
-    got, grad_ref, maps_ref, query_ref, back, below_every, every, ret_a, ret_b, get_a, get_b,
-    first, cot, tiles, fine, other, terms, slots, partial, sibling, raw, pown,
+    fine, terms, back, every, ret_a, ret_b, get_a, get_b,
+    first, cot, tiles, other, got, slots, partial, sibling, raw, pown, pbuf,
     up_a, down_a, up_b, down_b, red_a, red_b, mid_a, mid_b, last_a, last_b, coarse, running,
     send, recv, local
 ):
@@ -225,15 +225,11 @@
     below = ((clip + 3) % 4, space)
     move_tiles = remote(frames, tiles, below)
     end_tiles = here(tail, tiles)
-    pool_tail = here(tail, slots.at[pl.ds(0, TILES)])
+    move_pool = remote(pown, pbuf, below)
 
     @pl.when(at_end)
     def _():
         end_tiles.start()
-
-    @pl.when(clip == 0)
-    def _():
-        pool_tail.start()
 
     barrier = pltpu.get_barrier_semaphore()
     greeted = [along_x(d, k) for d in range(1, NX) for k in range(NC)]
@@ -254,27 +250,6 @@
         for b in range(BLK):
             target[b] = dot(perm_ref[...], raw[b]).astype(BF16)
 
-    @pl.when(clip > 0)
-    def _():
-        move_tiles.start()
-
-    load[0].wait()
-
-    @pl.when(clip > 0)
-    def _():
-        pool(first, pown)
-
-    @pl.when(clip == 0)
-    def _():
-        pool_tail.wait()
-        pool(slots, pown)
-
-    top, bottom = pl.ds(0, HALF), pl.ds(HALF, HALF)
-    keep_pool = start([here(pown, every.at[c, x, z])])
-    pool_a1 = start([remote(pown.at[:, top], every.at[c, x, z, :, top], along_x(d)) for d in range(1, NX)])
-    pool_b1 = start([remote(pown.at[:, bottom], every.at[c, x, z, :, bottom], along_z(d)) for d in range(1, NZ)])
-    sent += pool_a1 + pool_b1
-
     def products(begin, end, level, keep, put):
         def one(n, carry):
             for q in (2 * n, 2 * n + 1):
@@ -284,8 +259,33 @@
             return carry
         lax.fori_loop(begin // 2, end // 2, one, 0)
 
+    load[0].wait()
+    pool(first, pown)
+
+    @pl.when(clip > 0)
+    def _():
+        move_pool.start()
+        move_tiles.start()
+
+    @pl.when(at_end)
+    def _():
+        end_tiles.wait()
+        pool(tiles, pbuf)
+
     load[1].wait()
-    products(0, TILES // 2, 0, fine, terms)
+    products(0, TILES // 4, 0, fine, terms)
+
+    @pl.when(clip < 3)
+    def _():
+        move_pool.wait_recv()
+
+    top, bottom = pl.ds(0, HALF), pl.ds(HALF, HALF)
+    keep_pool = start([here(pbuf, every.at[c, x, z])])
+    pool_a1 = start([remote(pbuf.at[:, top], every.at[c, x, z, :, top], along_x(d)) for d in (2, 1, 3)])
+    pool_b1 = start([remote(pbuf.at[:, bottom], every.at[c, x, z, :, bottom], along_z(d)) for d in (2, 1, 3)])
+    sent += pool_a1 + pool_b1
+
+    products(TILES // 4, TILES // 2, 0, fine, terms)
 
     keep_pool[0].wait()
     arrive(pool_a1)
@@ -297,7 +297,6 @@
     sent += pool_a2 + pool_b2
 
     products(TILES // 2, TILES, 0, fine, terms)
-    put_maps = start([here(fine, maps_ref)])
 
     def fill_slots(half, source, row):
         def one(n, carry):
@@ -311,13 +310,13 @@
     def first_hop(source, row, into_a, into_b):
         fill_slots(0, source, row)
         stay_a = start([here(group(0, x), into_a.at[:, x])])
-        hop_a = start([remote(group(0, (x + d) % NX), into_a.at[:, x], along_x(d)) for d in range(1, NX)])
+        hop_a = start([remote(group(0, (x + d) % NX), into_a.at[:, x], along_x(d)) for d in (2, 1, 3)])
         fill_slots(1, source, row)
         stay_b = start([here(group(1, z), into_b.at[:, z])])
-        hop_b = start([remote(group(1, (z + d) % NZ), into_b.at[:, z], along_z(d)) for d in range(1, NZ)])
+        hop_b = start([remote(group(1, (z + d) % NZ), into_b.at[:, z], along_z(d)) for d in (2, 1, 3)])
         return stay_a, hop_a, stay_b, hop_b
 
-    others = [(d, k) for d in range(NZ) for k in range(NC) if d or k]
+    others = [(2, 0), (2, 1), (1, 0), (3, 0), (1, 1), (3, 1), (0, 1)]
 
     def second_hop(hops, from_a, from_b, into):
         stay_a, hop_a, stay_b, hop_b = hops
@@ -411,8 +410,8 @@
         return carry
 
     lax.fori_loop(0, NX * BLK, middle, 0)
-    red_a2 = start([remote(mid_a.at[(x + d) % NX], last_a.at[x], along_x(d)) for d in range(1, NX)])
-    red_b2 = start([remote(mid_b.at[(z + d) % NZ], last_b.at[z], along_z(d)) for d in range(1, NZ)])
+    red_a2 = start([remote(mid_a.at[(x + d) % NX], last_a.at[x], along_x(d)) for d in (2, 1, 3)])
+    red_b2 = start([remote(mid_b.at[(z + d) % NZ], last_b.at[z], along_z(d)) for d in (2, 1, 3)])
     sent += red_a2 + red_b2
     last_a[x] = mid_a[x]
     last_b[z] = mid_b[z]
@@ -420,10 +419,6 @@
     for copy in ret_hops[1] + ret_hops[3]:
         copy.wait_send()
 
-    @pl.when(at_end)
-    def _():
-        end_tiles.wait()
-
     @pl.when(clip < 3)
     def _():
         move_tiles.wait_recv()
@@ -432,7 +427,8 @@
 
     arrive(pool_a3)
     arrive(pool_b3)
-    pool_4 = start([remote(every.at[c], below_every.at[c], below)])
+    pool_4 = start([remote(every.at[c], every.at[c], along_x(0, 1))])
+    sent += pool_4
 
     def total(buffer, at):
         value = buffer[(0, *at)].astype(F32)
@@ -449,13 +445,24 @@
     for b in range(BLK):
         raw[b] = lax.dot_general(perm_ref[...], coarse[b], flip, preferred_element_type=F32).astype(BF16)
 
+    for copy in share + red_1 + red_2:
+        copy.wait_send()
+    arrive(pool_4)
+    load_every = start([here(every, partial)])
+    load_every[0].wait()
+
+    def query(n, carry):
+        for t in range(4):
+            m = 4 * n + t
+            at = table[CTILE, m]
+            tile = partial[at // (NX * NZ * BLK), (at // (NZ * BLK)) % NX, (at // BLK) % NZ, at % BLK]
+            other[m] = (dot(other[m], tile) * scale).astype(BF16)
+        return carry
+
+    lax.fori_loop(0, TILES // 4, query, 0)
+
     get_far, near = second_hop(get_hops, get_a, get_b, got)
     sent += get_far
-    stay += near
-
-    arrive(pool_4)
-    pool_5 = start([remote(below_every.at[c], below_every.at[c], along_x(0, 1))])
-    sent += pool_4 + pool_5
 
     arrive(ret_far)
     for copy in get_hops[1] + get_hops[3]:
@@ -468,45 +475,44 @@
         rows = pl.ds(part * 64, 64)
         running[0] = jnp.zeros((64, PIX), F32)
 
-        def add(n, carry):
-            running[n + 1] = running[n] + slots[table[ORDER, n], rows].astype(F32)
+        def add(n, value):
+            for m in (4 * n, 4 * n + 1, 4 * n + 2, 4 * n + 3):
+                value = value + slots[table[ORDER, m], rows].astype(F32)
+                running[m + 1] = value
+            return value
+
+        lax.fori_loop(0, SLOTS // 4, add, jnp.zeros((64, PIX), F32))
+
+        def gradient(n, carry):
+            for t in range(8):
+                m = 8 * n + t
+                at = pl.ds(pl.multiple_of((m % 16) * SIDE, SIDE), SIDE)
+                value = dot(widen_ref[rows], raw[m // 16, at]) * scale
+                value = value + (running[table[FIRST, m + 1]] - running[table[FIRST, m]])
+                terms[m, rows] = value.astype(BF16)
             return carry
 
-        lax.fori_loop(0, SLOTS, add, 0)
-
-        def gradient(n, carry):
-            at = pl.ds(pl.multiple_of((n % 16) * SIDE, SIDE), SIDE)
-            value = dot(widen_ref[rows], raw[n // 16, at]) * scale
-            value = value + (running[table[FIRST, n + 1]] - running[table[FIRST, n]])
-            terms[n, rows] = value.astype(BF16)
-            return carry
-
-        lax.fori_loop(0, TILES, gradient, 0)
-    put = start([here(terms, grad_ref)])
-
-    for copy in share + red_1 + red_2:
-        copy.wait_send()
-    arrive(pool_5)
-    load_every = start([here(below_every, partial)])
-    load_every[0].wait()
-
-    def query(n, carry):
-        at = table[CTILE, n]
-        tile = partial[at // (NX * NZ * BLK), (at // (NZ * BLK)) % NX, (at // BLK) % NZ, at % BLK]
-        other[n] = (dot(other[n], tile) * scale).astype(BF16)
+        lax.fori_loop(0, TILES // 8, gradient, 0)
+
+    arrive(get_far)
+    for copy in near:
+        copy.wait()
+
+    def last(n, carry):
+        for t in range(4):
+            m = 4 * n + t
+            value = dot(fine[m], got[table[GOT, m]]) * scale
+            fine[m] = (value + other[m].astype(F32)).astype(BF16)
         return carry
 
-    lax.fori_loop(0, TILES, query, 0)
-    put += start([here(other, query_ref)])
-
-    arrive(get_far)
-    for copy in put + put_maps:
-        copy.wait()
+    lax.fori_loop(0, TILES // 4, last, 0)
+
     for copy in sent:
         copy.wait_send()
 
     @pl.when(clip > 0)
     def _():
+        move_pool.wait_send()
         move_tiles.wait_send()
 
 
@@ -521,17 +527,15 @@
     outs = pl.pallas_call(
         exchange_kernel,
         in_specs=[smem] + [vmem] * 6 + [hbm] * 3,
-        out_specs=[hbm] * 11,
+        out_specs=[vmem] * 2 + [hbm] * 6,
         out_shape=[
-            shape(SLOTS), shape(TILES), shape(TILES), shape(TILES), shape(SLOTS),
-            shape(NC, NX, NZ, BLK), shape(NC, NX, NZ, BLK),
+            full(TILES), full(TILES), shape(SLOTS), shape(NC, NX, NZ, BLK),
             shape(8, NX), shape(8, NZ), shape(8, NX), shape(8, NZ),
         ],
         scratch_shapes=[
             full(TILES + 1), pltpu.VMEM((TILES, 2, WIN * WIN, PIX), BF16),
-            full(TILES), full(TILES), full(TILES), full(TILES),
-            full(SLOTS), full(2, NX, NZ, BLK), full(NX, NZ, BLK),
-            full(BLK), full(BLK),
+            full(TILES), full(TILES), full(SLOTS), full(SLOTS),
+            full(2, NX, NZ, BLK), full(NX, NZ, BLK), full(BLK), full(BLK), full(BLK),
             half(2, BLK), half(2, BLK), half(2, BLK), half(2, BLK),
             half(2, NX, BLK), half(2, NZ, BLK), half(NX, BLK), half(NZ, BLK),
             half(NX, BLK), half(NZ, BLK), full(BLK), pltpu.VMEM((SLOTS + 1, 64, PIX), F32),
@@ -539,46 +543,16 @@
             pltpu.SemaphoreType.DMA((24,)),
         ],
         compiler_params=pltpu.CompilerParams(
-            collective_id=0, has_side_effects=True, vmem_limit_bytes=62 * 2**20),
+            collective_id=0, has_side_effects=True, vmem_limit_bytes=55 * 2**20),
         name="exchange",
     )(table, jnp.asarray(placement(), BF16), jnp.asarray(pool_rows(), BF16),
       jnp.asarray(block_rows(), BF16), jnp.asarray(pool_rows().T, BF16), base, frac, frames, tail, cot)
-    return outs[:4]
-
-
-GROUP = 4
-
-
-def finish_kernel(table, maps_ref, query_ref, *refs):
-    for n in range(GROUP):
-        value = dot(maps_ref[n], refs[n][0]) * (1.0 / 16.0)
-        refs[GROUP][n] = (value + query_ref[n].astype(F32)).astype(BF16)
-
-
-def finish(table, maps, query, got):
-    tile = lambda q, t: (q, 0, 0)
-    block = pl.BlockSpec((GROUP, PIX, PIX), tile)
-    return pl.pallas_call(
-        finish_kernel,
-        grid_spec=pltpu.PrefetchScalarGridSpec(
-            num_scalar_prefetch=1,
-            grid=(TILES // GROUP,),
-            in_specs=[block, block] + [
-                pl.BlockSpec((1, PIX, PIX), lambda q, t, n=n: (t[GOT, q * GROUP + n], 0, 0))
-                for n in range(GROUP)
-            ],
-            out_specs=block,
-        ),
-        out_shape=jax.ShapeDtypeStruct((TILES, PIX, PIX), BF16),
-        compiler_params=pltpu.CompilerParams(vmem_limit_bytes=60 * 2**20),
-        name="finish",
-    )(table, maps, query, *[got] * GROUP)
+    return outs[:2]
 
 
 def body(frames, tail, cotangent, window_base, window_frac, fine_owner, fine_local, coarse_owner, coarse_block):
     table = plan(*(v.reshape(8, 128) for v in (fine_owner, fine_local, coarse_owner, coarse_block)))
-    got, grad_b, maps, query = exchange(table, frames[0], tail, cotangent[0], window_base[0], window_frac[0])
-    grad_a = finish(table, maps, query, got)
+    grad_a, grad_b = exchange(table, frames[0], tail, cotangent[0], window_base[0], window_frac[0])
     return grad_a[None], grad_b[None]
 
 

time: 294 us -> 268 us (0.912)
  Pallas kernels: 282 us -> 259 us
    pallas_call x1, Pallas kernels: 270 us -> 257 us  [exchange(): pl.pallas_call(exchange_kernel, in_specs=[smem] + [vmem] * 6 + [hbm] * 3,...]
    pallas_call x1 -> x0, Pallas kernels: 9.94 us -> none  [finish(): pl.pallas_call(finish_kernel, grid_spec=pltpu.PrefetchScalarGridSpec(num_...]
    unnamed x2 -> x3, local copies, waits for them, and re-layouts: 8.39 us -> 7.78 us
where the time goes in v3:
time: 268 us
  Pallas kernels  259 us (97%)
  local copies, waits for them, and re-layouts  7.78 us (3%)
    pallas_call x1, Pallas kernels, exchange(): pl.pallas_call(exchange_kernel, in_specs=[smem] + [vmem] * 6 + [hbm] * 3,...  257 us
    unnamed x3, local copies, waits for them, and re-layouts  7.78 us

profile of v3, /device:TPU:1, one launch (start us, length us, event | category | flops | bytes accessed | tf_op | source)
XLA Modules:
  0.0 267.8 jit_solution(8882786956169770227)
XLA Ops:
  0.6 2.1 plan.1.table
  2.8 3.8 %copy.17 = bf16[1,32,2,81,256]{4,3,2,1,0:T(8,128)(2,1)} copy(bf16[1,32,2,81,256]{4,2,3,1,0:T(2,128)(2,1)} %param.15) | data formatting | bytes 5308416 | tf_op args[2]
  6.5 257.2 %exchange.1 = (bf16[32,256,256]{2,1,0:T(8,128)(2,1)S(1)}, bf16[32,256,256]{2,1,0:T(8,128)(2,1)S(1)}, bf16[64,256,256]{2,1,0:T(8,128)(2,1)}, bf16[2,4,4,2,256,256...) custom-call(s32[8,64]{1,0:T(8,128)} %plan.1.table, ...), custom_call_target="tpu_custom_call" | custom-call | tf_op jit(solution)/shard_map/exchange/pallas_call | solution.py:527
  263.7 2.0 copy.20
  265.7 2.0 copy.21

commit v4 on v3

--- a/solution.py
+++ b/solution.py
@@ -127,7 +127,8 @@
     ox, oz, oc = parts(own_row)
     got_slot = jnp.where(rank_row == 0, (oz * NC + oc) * NX + ox, TILES + (ox * NC + oc) * NZ + oz)
     ox, oz, oc = parts(own_col)
-    ret_slot = jnp.where(rank_col == 0, own_col, TILES + (oz * NX + ox) * NC + oc)
+    cross = (oc + me) % NC * 4
+    ret_slot = jnp.where(rank_col == 0, ox * 8 + cross + oz, TILES + oz * 8 + cross + ox)
     filled = total(jnp.where(ret_slot == wide_lane, wide_sub, 0), axis=0)
 
     ctile_row, ctile_col = (
@@ -151,8 +152,9 @@
     (_, key0_row), (_, key1_row) = asked(turned(owner) == me, turned(local), (lane < sub).astype(F32), 0)
     (ask0, key0), (ask1, key1) = asked(owner == me, local, (sub < lane).astype(F32), 1)
     px, pz, pc = parts(wide_sub)
-    served = total(jnp.where(wide_lane == wide_sub, ask0, 0), axis=0)
-    served += total(jnp.where(wide_lane == TILES + (pz * NX + px) * NC + pc, ask1, 0), axis=0)
+    cross = (pc + me) % NC * 4
+    served = total(jnp.where(wide_lane == px * 8 + cross + pz, ask0, 0), axis=0)
+    served += total(jnp.where(wide_lane == TILES + pz * 8 + cross + px, ask1, 0), axis=0)
     key_row = total(jnp.where(wide_lane == (pz * NC + pc) * NX + px, key0, 0), axis=0)
     key_row += total(jnp.where(wide_lane == TILES + (px * NC + pc) * NZ + pz, key1, 0), axis=0)
     px, pz, pc = parts(tall_lane)
@@ -180,8 +182,8 @@
 
 def exchange_kernel(
     table, spread_ref, pool_ref, perm_ref, widen_ref, base, frac, frames, tail, cot_ref,
-    fine, terms, back, every, ret_a, ret_b, get_a, get_b,
-    first, cot, tiles, other, got, slots, partial, sibling, raw, pown, pbuf,
+    fine, terms, other, got, back, every, ret_a, ret_b, get_a, get_b,
+    first, cot, tiles, slots, partial, sibling, raw, pown, pbuf,
     up_a, down_a, up_b, down_b, red_a, red_b, mid_a, mid_b, last_a, last_b, coarse, running,
     send, recv, local
 ):
@@ -243,17 +245,19 @@
 
     def pool(source, target):
         def one(n, carry):
-            rows = pl.ds(pl.multiple_of((n % 16) * SIDE, SIDE), SIDE)
-            raw[n // 16, rows, :] = (dot(pool_ref[...], source[n]) * scale).astype(BF16)
+            for t in range(8):
+                m = n * 8 + t
+                rows = pl.ds(pl.multiple_of((m % 16) * SIDE, SIDE), SIDE)
+                raw[m // 16, rows, :] = (dot(pool_ref[...], source[m]) * scale).astype(BF16)
             return carry
-        lax.fori_loop(0, TILES, one, 0)
+        lax.fori_loop(0, TILES // 8, one, 0)
         for b in range(BLK):
             target[b] = dot(perm_ref[...], raw[b]).astype(BF16)
 
     def products(begin, end, level, keep, put):
         def one(n, carry):
             for q in (2 * n, 2 * n + 1):
-                weights = window_map(spread_ref[...], cot[q, level], base[q, level], frac[q, level])
+                weights = window_map(spread_ref[...], cot[q, :, level], base[q, level], frac[q, level])
                 put[q] = (dot(weights, first[q]) * scale).astype(BF16)
                 keep[q] = weights.T
             return carry
@@ -265,7 +269,6 @@
     @pl.when(clip > 0)
     def _():
         move_pool.start()
-        move_tiles.start()
 
     @pl.when(at_end)
     def _():
@@ -278,6 +281,10 @@
     @pl.when(clip < 3)
     def _():
         move_pool.wait_recv()
+
+    @pl.when(clip > 0)
+    def _():
+        move_tiles.start()
 
     top, bottom = pl.ds(0, HALF), pl.ds(HALF, HALF)
     keep_pool = start([here(pbuf, every.at[c, x, z])])
@@ -300,36 +307,44 @@
 
     def fill_slots(half, source, row):
         def one(n, carry):
-            slots[half * TILES + n] = source[table[row, half * TILES + n]]
+            for t in range(4):
+                m = half * TILES + n * 4 + t
+                slots[m] = source[table[row, m]]
             return carry
-        lax.fori_loop(0, TILES, one, 0)
-
-    def group(half, n):
-        return slots.at[pl.ds(half * TILES + n * 8, 8)]
+        lax.fori_loop(0, TILES // 4, one, 0)
+
+    def group(half, n, k):
+        return slots.at[pl.ds(half * TILES + n * 8 + k * 4, 4)]
 
     def first_hop(source, row, into_a, into_b):
-        fill_slots(0, source, row)
-        stay_a = start([here(group(0, x), into_a.at[:, x])])
-        hop_a = start([remote(group(0, (x + d) % NX), into_a.at[:, x], along_x(d)) for d in (2, 1, 3)])
-        fill_slots(1, source, row)
-        stay_b = start([here(group(1, z), into_b.at[:, z])])
-        hop_b = start([remote(group(1, (z + d) % NZ), into_b.at[:, z], along_z(d)) for d in (2, 1, 3)])
-        return stay_a, hop_a, stay_b, hop_b
-
-    others = [(2, 0), (2, 1), (1, 0), (3, 0), (1, 1), (3, 1), (0, 1)]
+        a, b = [], []
+        for half, into, at, along, hops in ((0, into_a, x, along_x, a), (1, into_b, z, along_z, b)):
+            fill_slots(half, source, row)
+            for k in range(NC):
+                part = into.at[pl.ds(k * 4, 4), at]
+                far = start([remote(group(half, (at + d) % 4, k), part, along(d)) for d in (2, 1, 3)])
+                hops.append((far, start([here(group(half, at, k), part)])))
+        return a, b
+
+    def first_sent(hops):
+        for far, _ in hops[0] + hops[1]:
+            for copy in far:
+                copy.wait_send()
 
     def second_hop(hops, from_a, from_b, into):
-        stay_a, hop_a, stay_b, hop_b = hops
         into_a = into.at[pl.ds((z * NC + c) * 4, 4)]
         into_b = into.at[pl.ds(TILES + (x * NC + c) * 4, 4)]
-        stay_a[0].wait()
-        arrive(hop_a)
-        far = start([remote(from_a.at[(z + d) % NZ * NC + (c + k) % NC], into_a, along_z(d, k)) for d, k in others])
-        near = start([here(from_a.at[z * NC + c], into_a)])
-        stay_b[0].wait()
-        arrive(hop_b)
-        far += start([remote(from_b.at[(x + d) % NX * NC + (c + k) % NC], into_b, along_x(d, k)) for d, k in others])
-        near += start([here(from_b.at[x * NC + c], into_b)])
+        far, near = [], []
+        for k in range(NC):
+            for hop, source, target, at, along in (
+                (hops[0][k], from_a, into_a, z, along_z), (hops[1][k], from_b, into_b, x, along_x)):
+                hop[1][0].wait()
+                arrive(hop[0])
+                far += start([remote(source.at[k * 4 + (at + d) % 4], target, along(d, k)) for d in (2, 1, 3)])
+                if k == 0:
+                    near += start([here(source.at[at], target)])
+                else:
+                    far += start([remote(source.at[4 + at], target, along(0, 1))])
         return far, near
 
     ret_hops = first_hop(terms, FILLED, ret_a, ret_b)
@@ -351,11 +366,13 @@
 
     def fill(which, core):
         def one(n, carry):
-            value = first[table[PICK_A, core * TILES + n]].astype(F32)
-            value = value + first[table[PICK_B, core * TILES + n]].astype(F32)
-            partial[which, n // (NZ * BLK), (n // BLK) % NZ, n % BLK] = value.astype(BF16)
+            for t in range(4):
+                m = 4 * n + t
+                value = first[table[PICK_A, core * TILES + m]].astype(F32)
+                value = value + first[table[PICK_B, core * TILES + m]].astype(F32)
+                partial[which, m // (NZ * BLK), (m // BLK) % NZ, m % BLK] = value.astype(BF16)
             return carry
-        lax.fori_loop(0, TILES, one, 0)
+        lax.fori_loop(0, TILES // 4, one, 0)
 
     fill(1, 1 - c)
     share = start([remote(partial.at[1], sibling, along_x(0, 1))])
@@ -363,12 +380,14 @@
     arrive(share)
 
     def join(n, carry):
-        at = (n // (NZ * BLK), (n // BLK) % NZ, n % BLK)
-        mine = partial[(0, *at)].astype(F32)
-        partial[(0, *at)] = (mine + sibling[at].astype(F32)).astype(BF16)
+        for t in range(4):
+            m = 4 * n + t
+            at = (m // (NZ * BLK), (m // BLK) % NZ, m % BLK)
+            mine = partial[(0, *at)].astype(F32)
+            partial[(0, *at)] = (mine + sibling[at].astype(F32)).astype(BF16)
         return carry
 
-    lax.fori_loop(0, TILES, join, 0)
+    lax.fori_loop(0, TILES // 4, join, 0)
 
     mine = partial.at[0]
     z_far, x_far = (z + 2) % NZ, (x + 2) % NX
@@ -416,8 +435,7 @@
     last_a[x] = mid_a[x]
     last_b[z] = mid_b[z]
 
-    for copy in ret_hops[1] + ret_hops[3]:
-        copy.wait_send()
+    first_sent(ret_hops)
 
     @pl.when(clip < 3)
     def _():
@@ -465,8 +483,7 @@
     sent += get_far
 
     arrive(ret_far)
-    for copy in get_hops[1] + get_hops[3]:
-        copy.wait_send()
+    first_sent(get_hops)
     for copy in stay:
         copy.wait()
     load_back = start([here(back, slots)])
@@ -497,16 +514,6 @@
     arrive(get_far)
     for copy in near:
         copy.wait()
-
-    def last(n, carry):
-        for t in range(4):
-            m = 4 * n + t
-            value = dot(fine[m], got[table[GOT, m]]) * scale
-            fine[m] = (value + other[m].astype(F32)).astype(BF16)
-        return carry
-
-    lax.fori_loop(0, TILES // 4, last, 0)
-
     for copy in sent:
         copy.wait_send()
 
@@ -527,32 +534,66 @@
     outs = pl.pallas_call(
         exchange_kernel,
         in_specs=[smem] + [vmem] * 6 + [hbm] * 3,
-        out_specs=[vmem] * 2 + [hbm] * 6,
+        out_specs=[vmem] * 4 + [hbm] * 6,
         out_shape=[
-            full(TILES), full(TILES), shape(SLOTS), shape(NC, NX, NZ, BLK),
+            full(TILES), full(TILES), full(TILES), full(SLOTS), shape(SLOTS), shape(NC, NX, NZ, BLK),
             shape(8, NX), shape(8, NZ), shape(8, NX), shape(8, NZ),
         ],
         scratch_shapes=[
-            full(TILES + 1), pltpu.VMEM((TILES, 2, WIN * WIN, PIX), BF16),
-            full(TILES), full(TILES), full(SLOTS), full(SLOTS),
+            full(TILES + 1), pltpu.VMEM((TILES, WIN * WIN, 2, PIX), BF16),
+            full(TILES), full(SLOTS),
             full(2, NX, NZ, BLK), full(NX, NZ, BLK), full(BLK), full(BLK), full(BLK),
             half(2, BLK), half(2, BLK), half(2, BLK), half(2, BLK),
             half(2, NX, BLK), half(2, NZ, BLK), half(NX, BLK), half(NZ, BLK),
             half(NX, BLK), half(NZ, BLK), full(BLK), pltpu.VMEM((SLOTS + 1, 64, PIX), F32),
-            pltpu.SemaphoreType.DMA((80,)), pltpu.SemaphoreType.DMA((80,)),
-            pltpu.SemaphoreType.DMA((24,)),
+            pltpu.SemaphoreType.DMA((100,)), pltpu.SemaphoreType.DMA((100,)),
+            pltpu.SemaphoreType.DMA((32,)),
         ],
         compiler_params=pltpu.CompilerParams(
-            collective_id=0, has_side_effects=True, vmem_limit_bytes=55 * 2**20),
+            collective_id=0, has_side_effects=True, vmem_limit_bytes=43 * 2**20),
         name="exchange",
     )(table, jnp.asarray(placement(), BF16), jnp.asarray(pool_rows(), BF16),
       jnp.asarray(block_rows(), BF16), jnp.asarray(pool_rows().T, BF16), base, frac, frames, tail, cot)
-    return outs[:2]
+    return outs[:4]
+
+
+def finish_kernel(table, fine, terms, other, got, grad_a, grad_b, ready, done):
+    second = pltpu.make_async_copy(terms, grad_b, done.at[TILES // GROUP])
+    second.start()
+    copies = []
+    for g in range(TILES // GROUP):
+        for n in range(g * GROUP, (g + 1) * GROUP):
+            value = dot(fine[n], got[table[GOT, n]]) * (1.0 / 16.0)
+            ready[n] = (value + other[n].astype(F32)).astype(BF16)
+        rows = pl.ds(g * GROUP, GROUP)
+        copies.append(pltpu.make_async_copy(ready.at[rows], grad_a.at[rows], done.at[g]))
+        copies[-1].start()
+    for copy in copies:
+        copy.wait()
+    second.wait()
+
+
+GROUP = 4
+
+
+def finish(table, *parts):
+    vmem = pl.BlockSpec(memory_space=pltpu.VMEM)
+    out = jax.ShapeDtypeStruct((TILES, PIX, PIX), BF16)
+    return pl.pallas_call(
+        finish_kernel,
+        in_specs=[pl.BlockSpec(memory_space=pltpu.SMEM)] + [vmem] * 4,
+        out_specs=[pl.BlockSpec(memory_space=pl.ANY)] * 2,
+        out_shape=[out, out],
+        scratch_shapes=[pltpu.VMEM((TILES, PIX, PIX), BF16), pltpu.SemaphoreType.DMA((TILES // GROUP + 1,))],
+        compiler_params=pltpu.CompilerParams(vmem_limit_bytes=30 * 2**20),
+        name="finish",
+    )(table, *parts)
 
 
 def body(frames, tail, cotangent, window_base, window_frac, fine_owner, fine_local, coarse_owner, coarse_block):
     table = plan(*(v.reshape(8, 128) for v in (fine_owner, fine_local, coarse_owner, coarse_block)))
-    grad_a, grad_b = exchange(table, frames[0], tail, cotangent[0], window_base[0], window_frac[0])
+    parts = exchange(table, frames[0], tail, cotangent[0].transpose(0, 2, 1, 3), window_base[0], window_frac[0])
+    grad_a, grad_b = finish(table, *parts)
     return grad_a[None], grad_b[None]
 
 

time: 268 us -> 258 us (0.963)
  local copies, waits for them, and re-layouts: 7.78 us -> 0.01 us
    unnamed x3 -> x2, local copies, waits for them, and re-layouts: 7.78 us -> 0.01 us
    pallas_call x1, Pallas kernels: 257 us -> 251 us  [exchange(): pl.pallas_call(exchange_kernel, in_specs=[smem] + [vmem] * 6 + [hbm] * 3,...]
    pallas_call x0 -> x1, Pallas kernels: none -> 4.18 us  [finish(): pl.pallas_call(finish_kernel, in_specs=[pl.BlockSpec(memory_space=pltpu.S...]
where the time goes in v4:
time: 258 us
  Pallas kernels  257 us (100%)
    pallas_call x1, Pallas kernels, exchange(): pl.pallas_call(exchange_kernel, in_specs=[smem] + [vmem] * 6 + [hbm] * 3,...  251 us

profile of v4, /device:TPU:1, one launch (start us, length us, event | category | flops | bytes accessed | tf_op | source)
XLA Modules:
  0.0 257.8 jit_solution(1401999607291226886)
XLA Ops:
  0.6 2.1 plan.1.table
  2.8 0.0 copy-start
  2.8 250.8 %exchange.1 = (bf16[32,256,256]{2,1,0:T(8,128)(2,1)S(1)}, bf16[32,256,256]{2,1,0:T(8,128)(2,1)S(1)}, bf16[32,256,256]{2,1,0:T(8,128)(2,1)S(1)}, bf16[64,256,256]...) custom-call(s32[8,64]{1,0:T(8,128)} %plan.1.table, ...), custom_call_target="tpu_custom_call" | custom-call | tf_op jit(solution)/shard_map/exchange/pallas_call | solution.py:534
  253.6 0.0 copy-done
  253.6 4.2 %finish.1 = (bf16[32,256,256]{2,1,0:T(8,128)(2,1)}, bf16[32,256,256]{2,1,0:T(8,128)(2,1)}) custom-call(s32[8,64]{1,0:T(8,128)S(1)} %copy-done, bf16[32,256,256]{2,1,0:T(8,128)(2,1)S(1)} %get-tuple-element.8.fine, bf16[32,256,256]{2,1,0:T(8,128)(2,1)S(1)} %get-tuple-element.9.terms, bf16[32,256,256]{2,1,0:T(8,128)(2,1)S(1)} %get-tuple-element.10.other, ...), custom_call_target="tpu_custom_call" | custom-call | tf_op jit(solution)/shard_map/finish/pallas_call | solution.py:582
Async XLA Ops:
  2.8 250.8 %copy-start = (s32[8,64]{1,0:T(8,128)S(1)}, s32[8,64]{1,0:T(8,128)}, u32[]{:S(2)}) copy-start(s32[8,64]{1,0:T(8,128)} %plan.1.table) | copy-start | bytes 6148

commit v5 on v4

--- a/solution.py
+++ b/solution.py
@@ -89,7 +89,7 @@
     return jnp.concatenate(groups, axis=0).astype(BF16)
 
 
-def plan_kernel(owner_ref, local_ref, c_owner_ref, c_block_ref, out_ref):
+def make_table(owner_ref, local_ref, c_owner_ref, c_block_ref, out_ref):
     me = lax.axis_index("space")
     total = functools.partial(jnp.sum, keepdims=True)
     sub, lane = (lax.broadcasted_iota(jnp.int32, (TILES, TILES), n) for n in range(2))
@@ -129,7 +129,7 @@
     ox, oz, oc = parts(own_col)
     cross = (oc + me) % NC * 4
     ret_slot = jnp.where(rank_col == 0, ox * 8 + cross + oz, TILES + oz * 8 + cross + ox)
-    filled = total(jnp.where(ret_slot == wide_lane, wide_sub, 0), axis=0)
+    filled = jnp.max(jnp.where(ret_slot == wide_lane, wide_sub, 0), axis=0, keepdims=True)
 
     ctile_row, ctile_col = (
         ((o % NC) * (NX * NZ) + o // NC) * BLK + b for o, b in zip(mine(c_owner), mine(c_block)))
@@ -165,26 +165,20 @@
     order = total(jnp.where(place == slot_lane, slot_sub, 0), axis=0)
     first = total(jnp.where(key_col < slot_lane, 1, 0), axis=0)
     out_ref[...] = jnp.zeros((8, SLOTS), jnp.int32)
-    for row, value in enumerate((served, filled, pick_a, pick_b, ctile_row, got_slot, order, first)):
-        out_ref[row : row + 1, : value.shape[1]] = value
+    rows = (served, filled, pick_a, pick_b, ctile_row, got_slot, order, first)
+    tops = (TILES - 1, TILES - 1, TILES, TILES, SLOTS - 1, SLOTS - 1, SLOTS - 1, SLOTS)
+    for row, (value, top) in enumerate(zip(rows, tops)):
+        out_ref[row : row + 1, : value.shape[1]] = jnp.clip(value, 0, top)
 
 
 SERVED, FILLED, PICK_A, PICK_B, CTILE, GOT, ORDER, FIRST = range(8)
 
 
-def plan(*ids):
-    vmem = pl.BlockSpec(memory_space=pltpu.VMEM)
-    return pl.pallas_call(
-        plan_kernel, in_specs=[vmem] * 4, out_specs=vmem,
-        out_shape=jax.ShapeDtypeStruct((8, SLOTS), jnp.int32), name="plan",
-    )(*ids)
-
-
 def exchange_kernel(
-    table, spread_ref, pool_ref, perm_ref, widen_ref, base, frac, frames, tail, cot_ref,
-    fine, terms, other, got, back, every, ret_a, ret_b, get_a, get_b,
-    first, cot, tiles, slots, partial, sibling, raw, pown, pbuf,
-    up_a, down_a, up_b, down_b, red_a, red_b, mid_a, mid_b, last_a, last_b, coarse, running,
+    owner, local_id, c_owner, c_block, spread_ref, pool_ref, perm_ref, widen_ref, base, frac, frames, tail, cot_ref,
+    fine, terms, other, got, rows_of, back, every, below_every, ret_a, ret_b, get_a, get_b,
+    first, cot, tiles, slots, partial, sibling, raw, pbuf,
+    up_a, down_a, up_b, down_b, red_a, red_b, mid_a, mid_b, last_a, last_b, coarse, running, table,
     send, recv, local
 ):
     scale = 1.0 / 16.0
@@ -227,11 +221,15 @@
     below = ((clip + 3) % 4, space)
     move_tiles = remote(frames, tiles, below)
     end_tiles = here(tail, tiles)
-    move_pool = remote(pown, pbuf, below)
+    pool_tail = here(tail, slots.at[pl.ds(0, TILES)])
 
     @pl.when(at_end)
     def _():
         end_tiles.start()
+
+    @pl.when(clip == 0)
+    def _():
+        pool_tail.start()
 
     barrier = pltpu.get_barrier_semaphore()
     greeted = [along_x(d, k) for d in range(1, NX) for k in range(NC)]
@@ -242,6 +240,10 @@
     pl.semaphore_wait(barrier, len(greeted))
 
     sent = []
+
+    @pl.when(clip > 0)
+    def _():
+        move_tiles.start()
 
     def pool(source, target):
         def one(n, carry):
@@ -264,27 +266,15 @@
         lax.fori_loop(begin // 2, end // 2, one, 0)
 
     load[0].wait()
-    pool(first, pown)
 
     @pl.when(clip > 0)
     def _():
-        move_pool.start()
-
-    @pl.when(at_end)
-    def _():
-        end_tiles.wait()
-        pool(tiles, pbuf)
-
-    load[1].wait()
-    products(0, TILES // 4, 0, fine, terms)
-
-    @pl.when(clip < 3)
-    def _():
-        move_pool.wait_recv()
-
-    @pl.when(clip > 0)
-    def _():
-        move_tiles.start()
+        pool(first, pbuf)
+
+    @pl.when(clip == 0)
+    def _():
+        pool_tail.wait()
+        pool(slots, pbuf)
 
     top, bottom = pl.ds(0, HALF), pl.ds(HALF, HALF)
     keep_pool = start([here(pbuf, every.at[c, x, z])])
@@ -292,7 +282,11 @@
     pool_b1 = start([remote(pbuf.at[:, bottom], every.at[c, x, z, :, bottom], along_z(d)) for d in (2, 1, 3)])
     sent += pool_a1 + pool_b1
 
-    products(TILES // 4, TILES // 2, 0, fine, terms)
+    make_table(owner, local_id, c_owner, c_block, rows_of)
+    load_table = start([here(rows_of, table)])
+    load[1].wait()
+    products(0, TILES // 2, 0, fine, terms)
+    load_table[0].wait()
 
     keep_pool[0].wait()
     arrive(pool_a1)
@@ -416,6 +410,10 @@
         remote(mine.at[x_down, :, :, bottom], red_b.at[1], along_x(NX - 1)),
     ])
 
+    arrive(pool_a3)
+    arrive(pool_b3)
+    pool_4 = start([remote(every.at[c], below_every.at[c], below)])
+
     ret_far, stay = second_hop(ret_hops, ret_a, ret_b, back)
     sent += ret_far
 
@@ -437,16 +435,15 @@
 
     first_sent(ret_hops)
 
+    @pl.when(at_end)
+    def _():
+        end_tiles.wait()
+
     @pl.when(clip < 3)
     def _():
         move_tiles.wait_recv()
 
     get_hops = first_hop(tiles, SERVED, get_a, get_b)
-
-    arrive(pool_a3)
-    arrive(pool_b3)
-    pool_4 = start([remote(every.at[c], every.at[c], along_x(0, 1))])
-    sent += pool_4
 
     def total(buffer, at):
         value = buffer[(0, *at)].astype(F32)
@@ -462,22 +459,6 @@
     flip = (((0,), (0,)), ((), ()))
     for b in range(BLK):
         raw[b] = lax.dot_general(perm_ref[...], coarse[b], flip, preferred_element_type=F32).astype(BF16)
-
-    for copy in share + red_1 + red_2:
-        copy.wait_send()
-    arrive(pool_4)
-    load_every = start([here(every, partial)])
-    load_every[0].wait()
-
-    def query(n, carry):
-        for t in range(4):
-            m = 4 * n + t
-            at = table[CTILE, m]
-            tile = partial[at // (NX * NZ * BLK), (at // (NZ * BLK)) % NX, (at // BLK) % NZ, at % BLK]
-            other[m] = (dot(other[m], tile) * scale).astype(BF16)
-        return carry
-
-    lax.fori_loop(0, TILES // 4, query, 0)
 
     get_far, near = second_hop(get_hops, get_a, get_b, got)
     sent += get_far
@@ -511,6 +492,25 @@
 
         lax.fori_loop(0, TILES // 8, gradient, 0)
 
+    arrive(pool_4)
+    pool_5 = start([remote(below_every.at[c], below_every.at[c], along_x(0, 1))])
+    sent += pool_4 + pool_5
+    for copy in share + red_1 + red_2:
+        copy.wait_send()
+    arrive(pool_5)
+    load_every = start([here(below_every, partial)])
+    load_every[0].wait()
+
+    def query(n, carry):
+        for t in range(4):
+            m = 4 * n + t
+            at = table[CTILE, m]
+            tile = partial[at // (NX * NZ * BLK), (at // (NZ * BLK)) % NX, (at // BLK) % NZ, at % BLK]
+            other[m] = (dot(other[m], tile) * scale).astype(BF16)
+        return carry
+
+    lax.fori_loop(0, TILES // 4, query, 0)
+
     arrive(get_far)
     for copy in near:
         copy.wait()
@@ -519,12 +519,10 @@
 
     @pl.when(clip > 0)
     def _():
-        move_pool.wait_send()
         move_tiles.wait_send()
 
 
-def exchange(table, frames, tail, cot, base, frac):
-    smem = pl.BlockSpec(memory_space=pltpu.SMEM)
+def exchange(ids, frames, tail, cot, base, frac):
     vmem = pl.BlockSpec(memory_space=pltpu.VMEM)
     hbm = pl.BlockSpec(memory_space=pl.ANY)
     tile = (PIX, PIX)
@@ -533,33 +531,38 @@
     full = lambda *s: pltpu.VMEM(s + tile, BF16)
     outs = pl.pallas_call(
         exchange_kernel,
-        in_specs=[smem] + [vmem] * 6 + [hbm] * 3,
-        out_specs=[vmem] * 4 + [hbm] * 6,
+        in_specs=[vmem] * 10 + [hbm] * 3,
+        out_specs=[vmem] * 5 + [hbm] * 7,
         out_shape=[
-            full(TILES), full(TILES), full(TILES), full(SLOTS), shape(SLOTS), shape(NC, NX, NZ, BLK),
+            full(TILES), full(TILES), full(TILES), full(SLOTS),
+            pltpu.VMEM((8, SLOTS), jnp.int32), shape(SLOTS), shape(NC, NX, NZ, BLK), shape(NC, NX, NZ, BLK),
             shape(8, NX), shape(8, NZ), shape(8, NX), shape(8, NZ),
         ],
         scratch_shapes=[
             full(TILES + 1), pltpu.VMEM((TILES, WIN * WIN, 2, PIX), BF16),
             full(TILES), full(SLOTS),
-            full(2, NX, NZ, BLK), full(NX, NZ, BLK), full(BLK), full(BLK), full(BLK),
+            full(2, NX, NZ, BLK), full(NX, NZ, BLK), full(BLK), full(BLK),
             half(2, BLK), half(2, BLK), half(2, BLK), half(2, BLK),
             half(2, NX, BLK), half(2, NZ, BLK), half(NX, BLK), half(NZ, BLK),
             half(NX, BLK), half(NZ, BLK), full(BLK), pltpu.VMEM((SLOTS + 1, 64, PIX), F32),
+            pltpu.SMEM((8, SLOTS), jnp.int32),
             pltpu.SemaphoreType.DMA((100,)), pltpu.SemaphoreType.DMA((100,)),
             pltpu.SemaphoreType.DMA((32,)),
         ],
         compiler_params=pltpu.CompilerParams(
             collective_id=0, has_side_effects=True, vmem_limit_bytes=43 * 2**20),
         name="exchange",
-    )(table, jnp.asarray(placement(), BF16), jnp.asarray(pool_rows(), BF16),
+    )(*ids, jnp.asarray(placement(), BF16), jnp.asarray(pool_rows(), BF16),
       jnp.asarray(block_rows(), BF16), jnp.asarray(pool_rows().T, BF16), base, frac, frames, tail, cot)
-    return outs[:4]
-
-
-def finish_kernel(table, fine, terms, other, got, grad_a, grad_b, ready, done):
+    return outs[:5]
+
+
+def finish_kernel(fine, terms, other, got, rows_of, grad_a, grad_b, ready, table, done):
     second = pltpu.make_async_copy(terms, grad_b, done.at[TILES // GROUP])
     second.start()
+    load = pltpu.make_async_copy(rows_of, table, done.at[TILES // GROUP + 1])
+    load.start()
+    load.wait()
     copies = []
     for g in range(TILES // GROUP):
         for n in range(g * GROUP, (g + 1) * GROUP):
@@ -576,24 +579,26 @@
 GROUP = 4
 
 
-def finish(table, *parts):
+def finish(*parts):
     vmem = pl.BlockSpec(memory_space=pltpu.VMEM)
     out = jax.ShapeDtypeStruct((TILES, PIX, PIX), BF16)
     return pl.pallas_call(
         finish_kernel,
-        in_specs=[pl.BlockSpec(memory_space=pltpu.SMEM)] + [vmem] * 4,
+        in_specs=[vmem] * 5,
         out_specs=[pl.BlockSpec(memory_space=pl.ANY)] * 2,
         out_shape=[out, out],
-        scratch_shapes=[pltpu.VMEM((TILES, PIX, PIX), BF16), pltpu.SemaphoreType.DMA((TILES // GROUP + 1,))],
-        compiler_params=pltpu.CompilerParams(vmem_limit_bytes=30 * 2**20),
+        scratch_shapes=[
+            pltpu.VMEM((TILES, PIX, PIX), BF16), pltpu.SMEM((8, SLOTS), jnp.int32),
+            pltpu.SemaphoreType.DMA((TILES // GROUP + 2,))],
+        compiler_params=pltpu.CompilerParams(vmem_limit_bytes=12 * 2**20),
         name="finish",
-    )(table, *parts)
+    )(*parts)
 
 
 def body(frames, tail, cotangent, window_base, window_frac, fine_owner, fine_local, coarse_owner, coarse_block):
-    table = plan(*(v.reshape(8, 128) for v in (fine_owner, fine_local, coarse_owner, coarse_block)))
-    parts = exchange(table, frames[0], tail, cotangent[0].transpose(0, 2, 1, 3), window_base[0], window_frac[0])
-    grad_a, grad_b = finish(table, *parts)
+    ids = [v.reshape(8, 128) for v in (fine_owner, fine_local, coarse_owner, coarse_block)]
+    parts = exchange(ids, frames[0], tail, cotangent[0].transpose(0, 2, 1, 3), window_base[0], window_frac[0])
+    grad_a, grad_b = finish(*parts)
     return grad_a[None], grad_b[None]
 
 

time: 258 us -> 249 us (0.965)
  Pallas kernels: 257 us -> 248 us
    pallas_call x3 -> x2, Pallas kernels: 257 us -> 248 us  [the longest x1 245 us: exchange(): pl.pallas_call(exchange_kernel, in_specs=[vmem] * 10 + [hbm] * 3, out_spe...]
where the time goes in v5:
time: 249 us
  Pallas kernels  248 us (100%)
    pallas_call x1, Pallas kernels, exchange(): pl.pallas_call(exchange_kernel, in_specs=[vmem] * 10 + [hbm] * 3, out_spe...  245 us

profile of v5, /device:TPU:1, one launch (start us, length us, event | category | flops | bytes accessed | tf_op | source)
XLA Modules:
  0.0 248.5 jit_solution(1221930247885094745)
XLA Ops:
  0.6 244.5 %exchange.1 = (bf16[32,256,256]{2,1,0:T(8,128)(2,1)S(1)}, bf16[32,256,256]{2,1,0:T(8,128)(2,1)S(1)}, bf16[32,256,256]{2,1,0:T(8,128)(2,1)S(1)}, bf16[64,256,256]...) custom-call(s32[8,128]{1,0:T(8,128)} %bitcast.16, ...), custom_call_target="tpu_custom_call" | custom-call | tf_op jit(solution)/shard_map/exchange/pallas_call | solution.py:532
  245.2 3.4 %finish.1 = (bf16[32,256,256]{2,1,0:T(8,128)(2,1)}, bf16[32,256,256]{2,1,0:T(8,128)(2,1)}) custom-call(bf16[32,256,256]{2,1,0:T(8,128)(2,1)S(1)} %get-tuple-element.9.fine, bf16[32,256,256]{2,1,0:T(8,128)(2,1)S(1)} %get-tuple-element.10.terms, bf16[32,256,256]{2,1,0:T(8,128)(2,1)S(1)} %get-tuple-element.11.other, ...), custom_call_target="tpu_custom_call" | custom-call | tf_op jit(solution)/shard_map/finish/pallas_call | solution.py:585

commit v6 on v5

--- a/solution.py
+++ b/solution.py
@@ -178,7 +178,7 @@
     owner, local_id, c_owner, c_block, spread_ref, pool_ref, perm_ref, widen_ref, base, frac, frames, tail, cot_ref,
     fine, terms, other, got, rows_of, back, every, below_every, ret_a, ret_b, get_a, get_b,
     first, cot, tiles, slots, partial, sibling, raw, pbuf,
-    up_a, down_a, up_b, down_b, red_a, red_b, mid_a, mid_b, last_a, last_b, coarse, running, table,
+    up_a, down_a, up_b, down_b, up_c, down_c, up_d, down_d, red_a, red_b, mid_a, mid_b, last_a, last_b, coarse, running, table,
     send, recv, local
 ):
     scale = 1.0 / 16.0
@@ -285,7 +285,7 @@
     make_table(owner, local_id, c_owner, c_block, rows_of)
     load_table = start([here(rows_of, table)])
     load[1].wait()
-    products(0, TILES // 2, 0, fine, terms)
+    products(0, TILES // 4, 0, fine, terms)
     load_table[0].wait()
 
     keep_pool[0].wait()
@@ -297,7 +297,7 @@
     pool_b2 = start([remote(line, line, along_x(d)) for d in (1, NX - 1)])
     sent += pool_a2 + pool_b2
 
-    products(TILES // 2, TILES, 0, fine, terms)
+    products(TILES // 4, TILES, 0, fine, terms)
 
     def fill_slots(half, source, row):
         def one(n, carry):
@@ -427,11 +427,12 @@
         return carry
 
     lax.fori_loop(0, NX * BLK, middle, 0)
-    red_a2 = start([remote(mid_a.at[(x + d) % NX], last_a.at[x], along_x(d)) for d in (2, 1, 3)])
-    red_b2 = start([remote(mid_b.at[(z + d) % NZ], last_b.at[z], along_z(d)) for d in (2, 1, 3)])
-    sent += red_a2 + red_b2
-    last_a[x] = mid_a[x]
-    last_b[z] = mid_b[z]
+    red_3 = start([
+        remote(mid_a.at[x_far, 0], up_c, along_x(1)),
+        remote(mid_a.at[x_far, 1], down_c, along_x(NX - 1)),
+        remote(mid_b.at[z_far, 0], up_d, along_z(1)),
+        remote(mid_b.at[z_far, 1], down_d, along_z(NZ - 1)),
+    ])
 
     first_sent(ret_hops)
 
@@ -445,23 +446,31 @@
 
     get_hops = first_hop(tiles, SERVED, get_a, get_b)
 
-    def total(buffer, at):
-        value = buffer[(0, *at)].astype(F32)
-        for n in range(1, 4):
-            value = value + buffer[(n, *at)].astype(F32)
-        return value
-
-    arrive(red_a2)
-    arrive(red_b2)
+    arrive(red_3)
+    for buffer, at, extra in (
+        (mid_a, (x_up, 0), up_c), (mid_a, (x_down, 1), down_c),
+        (mid_b, (z_up, 0), up_d), (mid_b, (z_down, 1), down_d),
+    ):
+        buffer[at] = (buffer[at].astype(F32) + extra[...].astype(F32)).astype(BF16)
+    red_4 = start([
+        remote(mid_a.at[x_up], last_a.at[0], along_x(1)),
+        remote(mid_a.at[x_down], last_a.at[1], along_x(NX - 1)),
+        remote(mid_b.at[z_up], last_b.at[0], along_z(1)),
+        remote(mid_b.at[z_down], last_b.at[1], along_z(NZ - 1)),
+    ])
+    sent += red_3 + red_4
+
+    get_far, near = second_hop(get_hops, get_a, get_b, got)
+    sent += get_far
+
+    arrive(red_4)
     for b in range(BLK):
-        coarse[b, top] = total(last_a, (b,)).astype(BF16)
-        coarse[b, bottom] = total(last_b, (b,)).astype(BF16)
+        for rows, buffer, at, extra in ((top, mid_a, x, last_a), (bottom, mid_b, z, last_b)):
+            value = buffer[at, b].astype(F32) + extra[0, b].astype(F32) + extra[1, b].astype(F32)
+            coarse[b, rows] = value.astype(BF16)
     flip = (((0,), (0,)), ((), ()))
     for b in range(BLK):
         raw[b] = lax.dot_general(perm_ref[...], coarse[b], flip, preferred_element_type=F32).astype(BF16)
-
-    get_far, near = second_hop(get_hops, get_a, get_b, got)
-    sent += get_far
 
     arrive(ret_far)
     first_sent(get_hops)
@@ -542,9 +551,9 @@
             full(TILES + 1), pltpu.VMEM((TILES, WIN * WIN, 2, PIX), BF16),
             full(TILES), full(SLOTS),
             full(2, NX, NZ, BLK), full(NX, NZ, BLK), full(BLK), full(BLK),
-            half(2, BLK), half(2, BLK), half(2, BLK), half(2, BLK),
+            half(2, BLK), half(2, BLK), half(2, BLK), half(2, BLK), half(), half(), half(), half(),
             half(2, NX, BLK), half(2, NZ, BLK), half(NX, BLK), half(NZ, BLK),
-            half(NX, BLK), half(NZ, BLK), full(BLK), pltpu.VMEM((SLOTS + 1, 64, PIX), F32),
+            half(2, BLK), half(2, BLK), full(BLK), pltpu.VMEM((SLOTS + 1, 64, PIX), F32),
             pltpu.SMEM((8, SLOTS), jnp.int32),
             pltpu.SemaphoreType.DMA((100,)), pltpu.SemaphoreType.DMA((100,)),
             pltpu.SemaphoreType.DMA((32,)),

time: 249 us -> 247 us (level)
  no operation moved by 1% of the time
where the time goes in v6:
time: 247 us
  Pallas kernels  247 us (100%)
    pallas_call x1, Pallas kernels, exchange(): pl.pallas_call(exchange_kernel, in_specs=[vmem] * 10 + [hbm] * 3, out_spe...  243 us

profile of v6, /device:TPU:1, one launch (start us, length us, event | category | flops | bytes accessed | tf_op | source)
XLA Modules:
  0.0 247.1 jit_solution(7700427741807455110)
XLA Ops:
  0.6 243.1 %exchange.1 = (bf16[32,256,256]{2,1,0:T(8,128)(2,1)S(1)}, bf16[32,256,256]{2,1,0:T(8,128)(2,1)S(1)}, bf16[32,256,256]{2,1,0:T(8,128)(2,1)S(1)}, bf16[64,256,256]...) custom-call(s32[8,128]{1,0:T(8,128)} %bitcast.16, ...), custom_call_target="tpu_custom_call" | custom-call | tf_op jit(solution)/shard_map/exchange/pallas_call | solution.py:541
  243.8 3.4 %finish.1 = (bf16[32,256,256]{2,1,0:T(8,128)(2,1)}, bf16[32,256,256]{2,1,0:T(8,128)(2,1)}) custom-call(bf16[32,256,256]{2,1,0:T(8,128)(2,1)S(1)} %get-tuple-element.9.fine, bf16[32,256,256]{2,1,0:T(8,128)(2,1)S(1)} %get-tuple-element.10.terms, bf16[32,256,256]{2,1,0:T(8,128)(2,1)S(1)} %get-tuple-element.11.other, ...), custom_call_target="tpu_custom_call" | custom-call | tf_op jit(solution)/shard_map/finish/pallas_call | solution.py:594

commit v7 on v6

--- a/solution.py
+++ b/solution.py
@@ -237,14 +237,6 @@
     greeted += [along_x(0, 1), ((clip + 1) % 4, space)]
     for device in greeted:
         pl.semaphore_signal(barrier, inc=1, device_id=device, device_id_type=MESH)
-    pl.semaphore_wait(barrier, len(greeted))
-
-    sent = []
-
-    @pl.when(clip > 0)
-    def _():
-        move_tiles.start()
-
     def pool(source, target):
         def one(n, carry):
             for t in range(8):
@@ -275,6 +267,14 @@
     def _():
         pool_tail.wait()
         pool(slots, pbuf)
+
+    pl.semaphore_wait(barrier, len(greeted))
+
+    sent = []
+
+    @pl.when(clip > 0)
+    def _():
+        move_tiles.start()
 
     top, bottom = pl.ds(0, HALF), pl.ds(HALF, HALF)
     keep_pool = start([here(pbuf, every.at[c, x, z])])

time: 247 us -> 247 us (level)
  no operation moved by 1% of the time
where the time goes in v7:
time: 247 us
  Pallas kernels  247 us (100%)
    pallas_call x1, Pallas kernels, exchange(): pl.pallas_call(exchange_kernel, in_specs=[vmem] * 10 + [hbm] * 3, out_spe...  243 us

profile of v7, /device:TPU:1, one launch (start us, length us, event | category | flops | bytes accessed | tf_op | source)
XLA Modules:
  0.0 247.2 jit_solution(15999019473770739141)
XLA Ops:
  0.6 243.1 %exchange.1 = (bf16[32,256,256]{2,1,0:T(8,128)(2,1)S(1)}, bf16[32,256,256]{2,1,0:T(8,128)(2,1)S(1)}, bf16[32,256,256]{2,1,0:T(8,128)(2,1)S(1)}, bf16[64,256,256]...) custom-call(s32[8,128]{1,0:T(8,128)} %bitcast.16, ...), custom_call_target="tpu_custom_call" | custom-call | tf_op jit(solution)/shard_map/exchange/pallas_call | solution.py:541
  243.8 3.4 %finish.1 = (bf16[32,256,256]{2,1,0:T(8,128)(2,1)}, bf16[32,256,256]{2,1,0:T(8,128)(2,1)}) custom-call(bf16[32,256,256]{2,1,0:T(8,128)(2,1)S(1)} %get-tuple-element.9.fine, bf16[32,256,256]{2,1,0:T(8,128)(2,1)S(1)} %get-tuple-element.10.terms, bf16[32,256,256]{2,1,0:T(8,128)(2,1)S(1)} %get-tuple-element.11.other, ...), custom_call_target="tpu_custom_call" | custom-call | tf_op jit(solution)/shard_map/finish/pallas_call | solution.py:594
